TPU v7x, 1024 devices: a whole 4x8x16 slice. The times are simulated.
1024 devices in a mesh: dp: 16 (over z_lo, core), fsdp: 64 (over z_hi, y, x).
Axes of the slice: x: 4, y: 8, z: 16 (z_hi: 2, z_lo: 8; z = z_hi * 8 + z_lo), core: 2. Of those that a mesh axis runs over, the one named last changes fastest.
Arguments:
- gradients: bfloat16 [16, 24576, 2048], P('dp', 'fsdp'), may hold values from -6 to 6
- master: float32 [24576, 2048], P('fsdp', 'dp'), may hold values from -1.3 to 1.3
- moment_one: float32 [24576, 2048], P('fsdp', 'dp'), may hold values from -4 to 4
- moment_two: float32 [24576, 2048], P('fsdp', 'dp'), may hold values from 0.01 to 0.1
- synced: bfloat16 [24576, 2048], P('fsdp', 'dp'), may hold values from -0.75 to 0.75
- rollout: bfloat16 [24576, 2048], P('fsdp', 'dp'), may hold values from -0.77 to 0.77
- amax_record: float32 [192, 16], P('fsdp', 'dp'), may hold values from 0.04 to 1.5
- row_table: int32 [128], replicated, may hold values from 0 to 63, as said below
- expert_owner: int32 [4], replicated, may hold values from 0 to 63
Outputs:
- new_master: float32 [24576, 2048], P('fsdp', 'dp')
- new_one: float32 [24576, 2048], P('fsdp', 'dp')
- new_two: float32 [24576, 2048], P('fsdp', 'dp')
- new_amax: float32 [192, 16], P('fsdp', 'dp')
- new_rollout: bfloat16 [24576, 2048], P('fsdp', 'dp')
Inputs may be any that keep to these rules, and one draw needn't show every extreme that they name: `row_table`: each of 0..63 appears exactly 2 times.
All inputs are finite; a program needn't handle non-finite values.
Results may differ from a plain program's by a relative error of at most 0.014.
Values may be sent and summed in bfloat16 or wider, within the bound.
No kernel may reach another device: no remote copies, remote signals or barrier semaphores. Data moves between devices by JAX's collectives and lax.ppermute only.
A program may use at most 32 MiB of HBM per device.

v0:
```python
import jax
import jax.numpy as jnp
from jax import lax
from jax.sharding import PartitionSpec as P

D = 7168
TILE = 128


beta_one = 0.9
beta_two = 0.95
bias_one = 1.0 - 0.9**10
bias_two = 1.0 - 0.95**10
step_size = 0.05
weight_decay = 0.1
adam_floor = 1e-08
code_limit = 448.0


def adam_step(master, moment_one, moment_two, gradient):
    new_one = beta_one * moment_one + (1.0 - beta_one) * gradient
    new_two = beta_two * moment_two + (1.0 - beta_two) * gradient * gradient
    update = new_one / bias_one / (jnp.sqrt(new_two / bias_two) + adam_floor)
    new_master = master - step_size * (update + weight_decay * master)
    return (new_master, new_one, new_two)


def owner_rows(row_table, expert_owner, blocks, owner_count):
    per_owner = TILE // owner_count
    ordering = jnp.argsort(row_table, stable=True)
    experts = blocks * TILE // D
    shifts = expert_owner[experts]
    owners = jnp.arange(owner_count, dtype=jnp.int32)
    first_slot = (owners[None, :] - shifts[:, None]) % owner_count * per_owner
    return ordering[first_slot[:, :, None] + jnp.arange(per_owner, dtype=jnp.int32)[None, None, :]]


def body(
    gradients, master, moment_one, moment_two, synced, rollout, amax_record, row_table, expert_owner
):
    owner_count = lax.axis_size("fsdp")
    replica_count = lax.axis_size("dp")
    row_count, column_count = master.shape
    summed = lax.psum_scatter(
        gradients[0].astype(jnp.float32).astype(jnp.bfloat16), "dp", scatter_dimension=1, tiled=True
    ).astype(jnp.float32)
    new_master, new_one, new_two = adam_step(master, moment_one, moment_two, summed / replica_count)
    difference = new_master - synced.astype(jnp.float32)
    block_count = row_count // TILE
    tile_count = column_count // TILE
    tiled_delta = difference.reshape(block_count, TILE, tile_count, TILE)
    new_amax = jnp.max(jnp.abs(tiled_delta), axis=(1, 3))
    scales = amax_record / code_limit
    code_values = (
        jnp.clip(tiled_delta / scales[:, None, :, None], -code_limit, code_limit)
        .astype(jnp.bfloat16)
        .reshape(block_count, TILE, column_count)
    )
    blocks = lax.axis_index("fsdp") * block_count + jnp.arange(block_count, dtype=jnp.int32)
    chosen = owner_rows(row_table, expert_owner, blocks, owner_count)
    per_owner = TILE // owner_count
    ordered = code_values[jnp.arange(block_count, dtype=jnp.int32)[:, None, None], chosen]
    outgoing = jnp.transpose(ordered, (1, 0, 2, 3)).reshape(
        owner_count, block_count * per_owner, column_count
    )
    spread = jnp.broadcast_to(scales[None], (owner_count, block_count, tile_count))
    incoming, scales_in = (
        lax.all_to_all(outgoing, "fsdp", split_axis=0, concat_axis=0, tiled=True),
        lax.all_to_all(
            spread.astype(jnp.bfloat16), "fsdp", split_axis=0, concat_axis=0, tiled=True
        ).astype(spread.dtype),
    )
    restored = (
        incoming.reshape(owner_count, block_count, per_owner, tile_count, TILE).astype(jnp.float32)
        * scales_in[:, :, None, :, None]
    )
    new_rollout = (rollout.astype(jnp.float32) + restored.reshape(row_count, column_count)).astype(
        jnp.bfloat16
    )
    return (new_master, new_one, new_two, new_amax, new_rollout)


def solution(mesh):
    return jax.shard_map(
        body,
        mesh=mesh,
        in_specs=(
            P("dp", "fsdp", None),
            P("fsdp", "dp"),
            P("fsdp", "dp"),
            P("fsdp", "dp"),
            P("fsdp", "dp"),
            P("fsdp", "dp"),
            P("fsdp", "dp"),
            P(),
            P(),
        ),
        out_specs=(
            P("fsdp", "dp"),
            P("fsdp", "dp"),
            P("fsdp", "dp"),
            P("fsdp", "dp"),
            P("fsdp", "dp"),
        ),
        check_vma=False,
    )
```

profile of v0, /device:TPU:8, one launch (start us, length us, event | category | flops | bytes accessed | tf_op | source)
XLA Modules:
  0.0 176.7 jit_solution(15126112295832370710)
XLA Ops:
  7.2 2.6 %copy.29 = bf16[384,2048]{0,1:T(8,128)(2,1)} copy(bf16[384,2048]{1,0:T(8,128)(2,1)} %bitcast.27) | data formatting | bytes 3145728
  9.9 0.6 copy-done.6
  10.5 0.6 broadcast_in_dim.5
  11.1 27.5 %all-to-all-start.1 = ((bf16[64,3,1]{1,2,0:T(2,128)(2,1)}), bf16[64,3,1]{1,2,0:T(2,128)(2,1)S(1)}, u32[]{:S(2)}, u32[]{:S(2)}) async-start(bf16[64,3,1]{1,2,0:T(2,128)(2,1)} %broadcast_in_dim.5), calls=%async_computation.1 | async-start | bytes 65536 | tf_op jit(solution)/shard_map/all_to_all | solution.py:69
  38.6 0.6 gather_fusion
  39.4 0.1 compare_select_fusion.1
  39.5 0.1 reshape.171
  39.6 2.5 %sort.17 = (s32[128]{0:T(128)}, s32[128]{0:T(128)S(1)}) sort(s32[128]{0:T(128)S(1)} %copy-done.7, s32[128]{0:T(128)S(1)} %iota.24), dimensions={0}, to_apply=%region_3.4 | sort | flops 896 | bytes 2048 | tf_op jit(solution)/shard_map/jit(argsort)/sort | solution.py:30
  42.2 2.7 %gather_fusion.1 = s32[384]{0:T(512)S(1)} fusion(s32[128]{0:T(128)S(1)} %get-tuple-element.6, s32[1024]{0:T(1024)S(1)} %pad_clamp_fusion), kind=kCustom, calls=%fused_computation.1 | custom fusion | bytes 4608 | tf_op jit(solution)/shard_map/gather | solution.py:35
  44.9 0.1 gather.13
  45.1 0.1 reshape.177
  45.2 85.0 %reduce-scatter.4.cloned.1.call-done = bf16[128,384]{1,0:T(8,128)(2,1)} async-done(((bf16[2048,384]{1,0:T(8,128)(2,1)}), bf16[128,384]{1,0:T(8,128)(2,1)}) %reduce-scatter.4.cloned.1.call-update) | async-done | bytes 98320
  130.2 1.0 copy.30
  131.2 1.0 abs_reduce_fusion
  132.3 3.2 %gather_fusion.2 = bf16[384,128]{1,0:T(8,128)(2,1)S(1)} fusion(bf16[3,128,128]{2,1,0:T(8,128)(2,1)S(1)} %clamp_convert_fusion, s32[384]{0:T(512)S(1)} %reshape.177), kind=kCustom, calls=%fused_computation.2 | custom fusion | bytes 199680 | tf_op jit(solution)/shard_map/gather | solution.py:62
  135.5 0.7 copy.26
  136.3 14.0 %all-to-all-start = ((bf16[64,6,128]{2,1,0:T(8,128)(2,1)}), bf16[64,6,128]{2,1,0:T(8,128)(2,1)S(1)}, u32[]{:S(2)}, u32[]{:S(2)}) async-start(bf16[64,6,128]{2,1,0:T(8,128)(2,1)} %copy.26), calls=%async_computation | async-start | bytes 262144 | tf_op jit(solution)/shard_map/all_to_all | solution.py:68
  150.3 0.1 copy.27
  150.4 0.1 copy.31
  150.5 0.1 mul.90
  150.6 0.2 mul.91
  150.8 0.6 bitcast_reduce_fusion
  151.4 17.6 %all-to-all-done = bf16[64,6,128]{2,1,0:T(8,128)(2,1)S(1)} async-done(((bf16[64,6,128]{2,1,0:T(8,128)(2,1)}), bf16[64,6,128]{2,1,0:T(8,128)(2,1)S(1)}, u32[]{:S(2)}, u32[]{:S(2)}) %all-to-all-start) | async-done | bytes 98336 | tf_op jit(solution)/shard_map/all_to_all | solution.py:68
  169.1 0.8 add_convert_fusion
  (28 shorter events, 0.4 us)
Async XLA Ops:
  7.2 31.5 %copy-start = (s32[4]{0:T(128)S(1)}, s32[4]{0:T(128)}, u32[]{:S(2)}) copy-start(s32[4]{0:T(128)} %param.17) | copy-start | bytes 52
  7.2 123.0 %reduce-scatter.4.cloned.1.call-start = ((), (), s32[]{:S(2)}) async-start(), calls=%async_computation.3 | async-start | bytes 1671168
  9.8 0.7 copy-start.6
  9.8 29.8 %copy-start.7 = (s32[128]{0:T(128)S(1)}, s32[128]{0:T(128)}, u32[]{:S(2)}) copy-start(s32[128]{0:T(128)} %param.16) | copy-start | bytes 1540
  11.1 125.1 %all-to-all-start.1 = ((bf16[64,3,1]{1,2,0:T(2,128)(2,1)}), bf16[64,3,1]{1,2,0:T(2,128)(2,1)S(1)}, u32[]{:S(2)}, u32[]{:S(2)}) async-start(bf16[64,3,1]{1,2,0:T(2,128)(2,1)} %broadcast_in_dim.5), calls=%async_computation.1 | async-start | bytes 65536 | tf_op jit(solution)/shard_map/all_to_all | solution.py:69
  42.2 89.0 %copy-start.1 = (f32[384,128]{1,0:T(8,128)S(1)}, f32[384,128]{1,0:T(8,128)}, u32[]{:S(2)}) copy-start(f32[384,128]{1,0:T(8,128)} %param.10) | copy-start | bytes 589828
  42.2 89.0 %copy-start.2 = (f32[384,128]{1,0:T(8,128)S(1)}, f32[384,128]{1,0:T(8,128)}, u32[]{:S(2)}) copy-start(f32[384,128]{1,0:T(8,128)} %param.11) | copy-start | bytes 589828
  42.2 89.1 %copy-start.3 = (f32[384,128]{1,0:T(8,128)S(1)}, f32[384,128]{1,0:T(8,128)}, u32[]{:S(2)}) copy-start(f32[384,128]{1,0:T(8,128)} %param.12) | copy-start | bytes 589828
  42.2 89.0 %copy-start.4 = (bf16[384,128]{1,0:T(8,128)(2,1)S(1)}, bf16[384,128]{1,0:T(8,128)(2,1)}, u32[]{:S(2)}) copy-start(bf16[384,128]{1,0:T(8,128)(2,1)} %param.13) | copy-start | bytes 294916
  132.2 36.8 %copy-start.5 = (bf16[384,128]{1,0:T(8,128)(2,1)S(1)}, bf16[384,128]{1,0:T(8,128)(2,1)}, u32[]{:S(2)}) copy-start(bf16[384,128]{1,0:T(8,128)(2,1)} %param.14) | copy-start | bytes 294916
  136.3 32.8 %all-to-all-start = ((bf16[64,6,128]{2,1,0:T(8,128)(2,1)}), bf16[64,6,128]{2,1,0:T(8,128)(2,1)S(1)}, u32[]{:S(2)}, u32[]{:S(2)}) async-start(bf16[64,6,128]{2,1,0:T(8,128)(2,1)} %copy.26), calls=%async_computation | async-start | bytes 262144 | tf_op jit(solution)/shard_map/all_to_all | solution.py:68
Sparse Core Ops, SparseCore 0:
  11.4 118.7 reduce-scatter.3
where the time goes:
time: 177 us
  waiting for transfers between devices  103 us (58%)
  starting transfers between devices  41.5 us (23%)
  between operations  14.2 us (8%)
  local copies, waits for them, and re-layouts  13.1 us (7%)
  other arithmetic  5.24 us (3%)
    unnamed x2, waiting for transfers between devices  85 us
    all_to_all x1, starting transfers between devices, body(): lax.all_to_all(spread.astype(jnp.bfloat16), 'fsdp', split_axis=0, concat_...  27.5 us
    all_to_all x1, waiting for transfers between devices, body(): lax.all_to_all(outgoing, 'fsdp', split_axis=0, concat_axis=0, tiled=True)  17.6 us
    all_to_all x1, starting transfers between devices, body(): lax.all_to_all(outgoing, 'fsdp', split_axis=0, concat_axis=0, tiled=True)  14 us
    unnamed x18, local copies, waits for them, and re-layouts  4.27 us
  transfers between devices with their start and end apart: 3, of which 2 were waited for; matrix products, arithmetic and copies ran while one was open for 8% of the time, Pallas kernels for 0%

commit v1 on v0

v1 whole, which is shorter than its diff:
```python
import jax
import jax.numpy as jnp
from jax import lax
from jax.sharding import PartitionSpec as P

D = 7168
TILE = 128

beta_one = 0.9
beta_two = 0.95
bias_one = 1.0 - 0.9**10
bias_two = 1.0 - 0.95**10
step_size = 0.05
weight_decay = 0.1
adam_floor = 1e-08


def adam_step(master, moment_one, moment_two, gradient):
    new_one = beta_one * moment_one + (1.0 - beta_one) * gradient
    new_two = beta_two * moment_two + (1.0 - beta_two) * gradient * gradient
    update = new_one / bias_one / (jnp.sqrt(new_two / bias_two) + adam_floor)
    new_master = master - step_size * (update + weight_decay * master)
    return (new_master, new_one, new_two)


def exchange(x, bit, replica_count):
    return lax.ppermute(x, "dp", [(i, i ^ bit) for i in range(replica_count)])


def half(x, index):
    return lax.dynamic_index_in_dim(x, index, axis=1, keepdims=False)


def wide(*terms):
    total = terms[0].astype(jnp.float32)
    for term in terms[1:]:
        total = total + term.astype(jnp.float32)
    return total


def body(
    gradients, master, moment_one, moment_two, synced, rollout, amax_record, row_table, expert_owner
):
    owner_count = lax.axis_size("fsdp")
    replica_count = lax.axis_size("dp")
    row_count, column_count = master.shape
    block_count = row_count // TILE
    per_owner = TILE // owner_count
    place = lax.axis_index("dp").astype(jnp.uint32)

    kept = gradients[0].reshape(row_count, replica_count // 2, 2, column_count).transpose(1, 2, 0, 3)
    core = place & 1
    terms = [half(kept, core)]
    received = exchange(half(kept, 1 - core), 1, replica_count)
    terms.append(received)
    bit = 2
    while bit < replica_count:
        mine = (place >> (bit.bit_length() - 1)) & 1
        pairs = [t.reshape(t.shape[0] // 2, 2, row_count, column_count) for t in terms]
        sending = wide(*[half(t, 1 - mine) for t in pairs]).astype(jnp.bfloat16)
        terms = [half(t, mine) for t in pairs]
        terms.append(exchange(sending, bit, replica_count))
        bit *= 2
    summed = wide(*[t[0] for t in terms])

    new_master, new_one, new_two = adam_step(master, moment_one, moment_two, summed / replica_count)
    difference = new_master - synced.astype(jnp.float32)
    tiled_delta = difference.reshape(block_count, TILE, TILE)
    new_amax = jnp.max(jnp.abs(tiled_delta), axis=(1, 2)).reshape(block_count, 1)
    limit = amax_record.reshape(block_count, 1, 1)
    clipped = jnp.clip(tiled_delta, -limit, limit).astype(jnp.bfloat16).reshape(row_count, column_count)

    rows = jnp.arange(TILE, dtype=jnp.int32)
    before = (row_table[None, :] < row_table[:, None]) | (
        (row_table[None, :] == row_table[:, None]) & (rows[None, :] < rows[:, None])
    )
    rank = jnp.sum(before.astype(jnp.int32), axis=1)
    blocks = jnp.arange(block_count, dtype=jnp.int32)
    experts = (lax.axis_index("fsdp") * block_count + blocks) * TILE // D
    shifts = expert_owner[experts]
    owner = (rank[None, :] // per_owner + shifts[:, None]) % owner_count
    slot = (owner * block_count + blocks[:, None]) * per_owner + rank[None, :] % per_owner
    chooser = (
        jnp.arange(row_count, dtype=jnp.int32)[:, None] == slot.reshape(1, row_count)
    ).astype(jnp.bfloat16)
    outgoing = lax.dot(chooser, clipped, preferred_element_type=jnp.float32).astype(jnp.bfloat16)
    incoming = lax.all_to_all(
        outgoing.reshape(owner_count * block_count, per_owner, column_count),
        "fsdp",
        split_axis=0,
        concat_axis=0,
        tiled=True,
    ).reshape(row_count, column_count)
    new_rollout = wide(rollout, incoming).astype(jnp.bfloat16)
    return (new_master, new_one, new_two, new_amax, new_rollout)


def solution(mesh):
    return jax.shard_map(
        body,
        mesh=mesh,
        in_specs=(
            P("dp", "fsdp", None),
            P("fsdp", "dp"),
            P("fsdp", "dp"),
            P("fsdp", "dp"),
            P("fsdp", "dp"),
            P("fsdp", "dp"),
            P("fsdp", "dp"),
            P(),
            P(),
        ),
        out_specs=(
            P("fsdp", "dp"),
            P("fsdp", "dp"),
            P("fsdp", "dp"),
            P("fsdp", "dp"),
            P("fsdp", "dp"),
        ),
        check_vma=False,
    )
```

time: 177 us -> 99 us (0.56)
  waiting for transfers between devices: 103 us -> 44.5 us
  between operations: 14.2 us -> 0.87 us
  local copies, waits for them, and re-layouts: 13.1 us -> 4.51 us
  starting transfers between devices: 41.5 us -> 44.9 us
  other arithmetic: 5.24 us -> 2.81 us
    unnamed x2 -> x0, waiting for transfers between devices: 85 us -> none
    ppermute x0 -> x4, waiting for transfers between devices: none -> 26.6 us  [exchange(): return lax.ppermute(x, 'dp', [(i, i ^ bit) for i in range(replica_count)])]
    ppermute x0 -> x4, starting transfers between devices: none -> 23.5 us  [exchange(): return lax.ppermute(x, 'dp', [(i, i ^ bit) for i in range(replica_count)])]
    all_to_all x2 -> x1, starting transfers between devices: 41.5 us -> 21.5 us  [body(): lax.all_to_all(outgoing.reshape(owner_count * block_count, per_owner, col...]
    gather x5 -> x1, local copies, waits for them, and re-layouts: 6.65 us -> 0.64 us  [body(): shifts = expert_owner[experts]]
    sort x1 -> x0, other arithmetic: 2.54 us -> none  [owner_rows(): ordering = jnp.argsort(row_table, stable=True)]
    unnamed x18 -> x19, local copies, waits for them, and re-layouts: 4.27 us -> 1.92 us
    dynamic_slice x0 -> x5, local copies, waits for them, and re-layouts: none -> 1.87 us  [half(): return lax.dynamic_index_in_dim(x, index, axis=1, keepdims=False)]
  transfers between devices with their start and end apart: 3 -> 5, of which waited for: 2 -> 5; matrix products, arithmetic and copies ran while one was open for 8% -> 2% of each run, Pallas kernels for 0% -> 0%
where the time goes in v1:
time: 99 us; the launch traced here: 98.6 us
  starting transfers between devices  44.9 us (45%)
  waiting for transfers between devices  44.5 us (45%)
  local copies, waits for them, and re-layouts  4.51 us (5%)
  other arithmetic  2.81 us (3%)
  matrix products  0.99 us (1%)
    ppermute x4, waiting for transfers between devices, exchange(): return lax.ppermute(x, 'dp', [(i, i ^ bit) for i in range(replica_count)])  26.6 us
    ppermute x4, starting transfers between devices, exchange(): return lax.ppermute(x, 'dp', [(i, i ^ bit) for i in range(replica_count)])  23.5 us
    all_to_all x1, starting transfers between devices, body(): lax.all_to_all(outgoing.reshape(owner_count * block_count, per_owner, col...  21.5 us
    all_to_all x1, waiting for transfers between devices, body(): lax.all_to_all(outgoing.reshape(owner_count * block_count, per_owner, col...  18 us
  transfers between devices with their start and end apart: 5, of which 5 were waited for; matrix products, arithmetic and copies ran while one was open for 2% of the time, Pallas kernels for 0%

profile of v1, /device:TPU:8, one launch (start us, length us, event | category | flops | bytes accessed | tf_op | source)
XLA Modules:
  0.0 98.6 jit_solution(6250169546986622011)
XLA Ops:
  0.7 1.9 %copy.17 = bf16[1,384,2048]{1,2,0:T(8,128)(2,1)S(1)} copy(bf16[1,384,2048]{2,1,0:T(8,128)(2,1)} %param.9) | data formatting | bytes 3145728 | tf_op args[0]
  2.5 0.2 dynamic-slice_bitcast_fusion.1
  2.8 1.2 %copy.19 = bf16[8,1,384,128]{3,2,0,1:T(8,128)(2,1)} copy(bf16[8,1,384,128]{2,3,1,0:T(8,128)(2,1)S(1)} %get-tuple-element.10) | data formatting | bytes 1572864 | tf_op jit(solution)/shard_map/jit(dynamic_index_in_dim)/dynamic_slice | solution.py:31
  3.9 1.9 %collective-permute-start = (bf16[8,384,128]{2,1,0:T(8,128)(2,1)}, bf16[8,384,128]{2,1,0:T(8,128)(2,1)S(1)}, u32[]{:S(2)}, u32[]{:S(2)}) collective-permute-start(bf16[8,384,128]{2,1,0:T(8,128)(2,1)} %bitcast.5), channel_id=1, source_target_pairs={{0,64},{64,0},{128,192},{192,128},{256,320},{320,256},{384,448},{4... | collective-permute-start | bytes 2359304 | tf_op jit(solution)/shard_map/ppermute | solution.py:27
  5.9 0.4 copy.18
  6.3 0.2 convert_reduce_fusion
  6.6 1.8 %collective-permute-done = bf16[8,384,128]{2,1,0:T(8,128)(2,1)S(1)} collective-permute-done((bf16[8,384,128]{2,1,0:T(8,128)(2,1)}, bf16[8,384,128]{2,1,0:T(8,128)(2,1)S(1)}, u32[]{:S(2)}, u32[]{:S(2)}) %collective-permute-start) | collective-permute-done | bytes 786464 | tf_op jit(solution)/shard_map/ppermute | solution.py:27
  8.3 0.1 fusion
  8.5 4.4 %collective-permute-start.1 = (bf16[4,384,128]{2,1,0:T(8,128)(2,1)S(1)}, bf16[4,384,128]{2,1,0:T(8,128)(2,1)S(1)}, u32[]{:S(2)}, u32[]{:S(2)}) collective-permute-start(bf16[4,384,128]{2,1,0:T(8,128)(2,1)S(1)} %fusion), channel_id=1, source_target_pairs={{0,128},{64,192},{128,0},{192,64},{256,384},{320,448},{384,256},{4... | collective-permute-start | bytes 1179656 | tf_op jit(solution)/shard_map/ppermute | solution.py:27
  12.9 0.6 gather_fusion
  13.6 0.1 fusion.13
  13.7 8.6 %collective-permute-done.1 = bf16[4,384,128]{2,1,0:T(8,128)(2,1)S(1)} collective-permute-done((bf16[4,384,128]{2,1,0:T(8,128)(2,1)S(1)}, bf16[4,384,128]{2,1,0:T(8,128)(2,1)S(1)}, u32[]{:S(2)}, u32[]{:S(2)}) %collective-permute-start.1) | collective-permute-done | bytes 393248 | tf_op jit(solution)/shard_map/ppermute | solution.py:27
  22.3 0.1 fusion.2
  22.4 6.2 %collective-permute-start.2 = (bf16[2,384,128]{2,1,0:T(8,128)(2,1)S(1)}, bf16[2,384,128]{2,1,0:T(8,128)(2,1)S(1)}, u32[]{:S(2)}, u32[]{:S(2)}) collective-permute-start(bf16[2,384,128]{2,1,0:T(8,128)(2,1)S(1)} %fusion.2), channel_id=1, source_target_pairs={{0,256},{64,320},{128,384},{192,448},{256,0},{320,64},{384,128},{4... | collective-permute-start | bytes 589832 | tf_op jit(solution)/shard_map/ppermute | solution.py:27
  28.6 8.9 %collective-permute-done.2 = bf16[2,384,128]{2,1,0:T(8,128)(2,1)S(1)} collective-permute-done((bf16[2,384,128]{2,1,0:T(8,128)(2,1)S(1)}, bf16[2,384,128]{2,1,0:T(8,128)(2,1)S(1)}, u32[]{:S(2)}, u32[]{:S(2)}) %collective-permute-start.2) | collective-permute-done | bytes 196640 | tf_op jit(solution)/shard_map/ppermute | solution.py:27
  37.6 10.9 %collective-permute-start.3 = (bf16[1,384,128]{2,1,0:T(8,128)(2,1)S(1)}, bf16[1,384,128]{2,1,0:T(8,128)(2,1)S(1)}, u32[]{:S(2)}, u32[]{:S(2)}) collective-permute-start(bf16[1,384,128]{2,1,0:T(8,128)(2,1)S(1)} %fusion.4), channel_id=1, source_target_pairs={{0,512},{64,576},{128,640},{192,704},{256,768},{320,832},{384,896}... | collective-permute-start | bytes 294920 | tf_op jit(solution)/shard_map/ppermute | solution.py:27
  48.5 0.1 broadcast_bitcast_fusion
  48.6 7.3 %collective-permute-done.3 = bf16[1,384,128]{2,1,0:T(8,128)(2,1)S(1)} collective-permute-done((bf16[1,384,128]{2,1,0:T(8,128)(2,1)S(1)}, bf16[1,384,128]{2,1,0:T(8,128)(2,1)S(1)}, u32[]{:S(2)}, u32[]{:S(2)}) %collective-permute-start.3) | collective-permute-done | bytes 98336 | tf_op jit(solution)/shard_map/ppermute | solution.py:27
  55.9 1.0 abs_reduce_fusion
  56.9 1.0 %convolution_convert_fusion = bf16[384,128]{1,0:T(8,128)(2,1)} fusion(s32[384]{0:T(512)S(1)} %fusion.13, f32[384,128]{1,0:T(8,128)S(1)} %get-tuple-element.6, bf16[384,128]{1,0:T(8,128)(2,1)S(1)} %copy-done.5, bf16[384]{0:T(512)(128)(2,1)S(1)} %get-tuple-element.13, bf16[384]{0:T(512)(128)(2,1)S(1)} %get-tuple-element.14), kind=kOutput, calls=%fused_computation.1 | convolution fusion | flops 38289408 | bytes 396288 | tf_op jit(solution)/shard_map/dot_general | solution.py:86
  57.9 21.5 %all-to-all-start = ((bf16[192,2,128]{2,1,0:T(2,128)(2,1)}), bf16[192,2,128]{2,1,0:T(2,128)(2,1)S(1)}, u32[]{:S(2)}, u32[]{:S(2)}) async-start(bf16[192,2,128]{2,1,0:T(2,128)(2,1)} %bitcast.24), calls=%async_computation | async-start | bytes 196608 | tf_op jit(solution)/shard_map/all_to_all | solution.py:87
  79.4 0.6 bitcast_reduce_fusion
  80.0 18.0 %all-to-all-done = bf16[192,2,128]{2,1,0:T(2,128)(2,1)S(1)} async-done(((bf16[192,2,128]{2,1,0:T(2,128)(2,1)}), bf16[192,2,128]{2,1,0:T(2,128)(2,1)S(1)}, u32[]{:S(2)}, u32[]{:S(2)}) %all-to-all-start) | async-done | bytes 98336 | tf_op jit(solution)/shard_map/all_to_all | solution.py:87
  98.0 0.7 fusion.3
  (25 shorter events, 0.2 us)
Async XLA Ops:
  0.6 12.3 %copy-start = (s32[4]{0:T(128)S(1)}, s32[4]{0:T(128)}, u32[]{:S(2)}) copy-start(s32[4]{0:T(128)} %param.17) | copy-start | bytes 52
  2.8 3.6 %copy-start.8 = (s32[128]{0:T(128)S(1)}, s32[128]{0:T(128)}, u32[]{:S(2)}) copy-start(s32[128]{0:T(128)} %param.16) | copy-start | bytes 1540
  3.9 4.4 %collective-permute-start = (bf16[8,384,128]{2,1,0:T(8,128)(2,1)}, bf16[8,384,128]{2,1,0:T(8,128)(2,1)S(1)}, u32[]{:S(2)}, u32[]{:S(2)}) collective-permute-start(bf16[8,384,128]{2,1,0:T(8,128)(2,1)} %bitcast.5), channel_id=1, source_target_pairs={{0,64},{64,0},{128,192},{192,128},{256,320},{320,256},{384,448},{4... | collective-permute-start | bytes 2359304 | tf_op jit(solution)/shard_map/ppermute | solution.py:27
  8.3 20.3 %copy-start.7 = (f32[3,1]{0,1:T(1,128)S(1)}, f32[3,1]{0,1:T(1,128)}, u32[]{:S(2)}) copy-start(f32[3,1]{0,1:T(1,128)} %param.15) | copy-start | bytes 40
  8.4 47.5 %copy-start.1 = (f32[384,128]{1,0:T(8,128)S(1)}, f32[384,128]{1,0:T(8,128)}, u32[]{:S(2)}) copy-start(f32[384,128]{1,0:T(8,128)} %param.10) | copy-start | bytes 589828
  8.4 47.5 %copy-start.2 = (f32[384,128]{1,0:T(8,128)S(1)}, f32[384,128]{1,0:T(8,128)}, u32[]{:S(2)}) copy-start(f32[384,128]{1,0:T(8,128)} %param.11) | copy-start | bytes 589828
  8.5 47.5 %copy-start.3 = (f32[384,128]{1,0:T(8,128)S(1)}, f32[384,128]{1,0:T(8,128)}, u32[]{:S(2)}) copy-start(f32[384,128]{1,0:T(8,128)} %param.12) | copy-start | bytes 589828
  8.5 47.4 %copy-start.5 = (bf16[384,128]{1,0:T(8,128)(2,1)S(1)}, bf16[384,128]{1,0:T(8,128)(2,1)}, u32[]{:S(2)}) copy-start(bf16[384,128]{1,0:T(8,128)(2,1)} %param.13) | copy-start | bytes 294916
  8.5 13.8 %collective-permute-start.1 = (bf16[4,384,128]{2,1,0:T(8,128)(2,1)S(1)}, bf16[4,384,128]{2,1,0:T(8,128)(2,1)S(1)}, u32[]{:S(2)}, u32[]{:S(2)}) collective-permute-start(bf16[4,384,128]{2,1,0:T(8,128)(2,1)S(1)} %fusion), channel_id=1, source_target_pairs={{0,128},{64,192},{128,0},{192,64},{256,384},{320,448},{384,256},{4... | collective-permute-start | bytes 1179656 | tf_op jit(solution)/shard_map/ppermute | solution.py:27
  22.4 75.6 %copy-start.6 = (bf16[384,128]{1,0:T(8,128)(2,1)S(1)}, bf16[384,128]{1,0:T(8,128)(2,1)}, u32[]{:S(2)}) copy-start(bf16[384,128]{1,0:T(8,128)(2,1)} %param.14) | copy-start | bytes 294916
  22.4 15.1 %collective-permute-start.2 = (bf16[2,384,128]{2,1,0:T(8,128)(2,1)S(1)}, bf16[2,384,128]{2,1,0:T(8,128)(2,1)S(1)}, u32[]{:S(2)}, u32[]{:S(2)}) collective-permute-start(bf16[2,384,128]{2,1,0:T(8,128)(2,1)S(1)} %fusion.2), channel_id=1, source_target_pairs={{0,256},{64,320},{128,384},{192,448},{256,0},{320,64},{384,128},{4... | collective-permute-start | bytes 589832 | tf_op jit(solution)/shard_map/ppermute | solution.py:27
  37.6 18.3 %collective-permute-start.3 = (bf16[1,384,128]{2,1,0:T(8,128)(2,1)S(1)}, bf16[1,384,128]{2,1,0:T(8,128)(2,1)S(1)}, u32[]{:S(2)}, u32[]{:S(2)}) collective-permute-start(bf16[1,384,128]{2,1,0:T(8,128)(2,1)S(1)} %fusion.4), channel_id=1, source_target_pairs={{0,512},{64,576},{128,640},{192,704},{256,768},{320,832},{384,896}... | collective-permute-start | bytes 294920 | tf_op jit(solution)/shard_map/ppermute | solution.py:27
  56.9 41.7 %copy-start.4 = (f32[384,128]{1,0:T(8,128)}, f32[384,128]{1,0:T(8,128)S(1)}, u32[]{:S(2)}) copy-start(f32[384,128]{1,0:T(8,128)S(1)} %get-tuple-element.6) | copy-start | bytes 589828
  57.9 40.1 %all-to-all-start = ((bf16[192,2,128]{2,1,0:T(2,128)(2,1)}), bf16[192,2,128]{2,1,0:T(2,128)(2,1)S(1)}, u32[]{:S(2)}, u32[]{:S(2)}) async-start(bf16[192,2,128]{2,1,0:T(2,128)(2,1)} %bitcast.24), calls=%async_computation | async-start | bytes 196608 | tf_op jit(solution)/shard_map/all_to_all | solution.py:87

commit v2 on v1

v2 whole, which is shorter than its diff:
```python
import functools

import jax
import jax.numpy as jnp
from jax import lax
from jax.experimental import pallas as pl
from jax.experimental.pallas import tpu as pltpu
from jax.sharding import PartitionSpec as P

D = 7168
TILE = 128
CHUNKS = 2

beta_one = 0.9
beta_two = 0.95
bias_one = 1.0 - 0.9**10
bias_two = 1.0 - 0.95**10
step_size = 0.05
weight_decay = 0.1
adam_floor = 1e-08

VMEM = pl.BlockSpec(memory_space=pltpu.VMEM)
ANY = pl.BlockSpec(memory_space=pl.ANY)
SMEM = pl.BlockSpec(memory_space=pltpu.SMEM)


def adam_step(master, moment_one, moment_two, gradient):
    new_one = beta_one * moment_one + (1.0 - beta_one) * gradient
    new_two = beta_two * moment_two + (1.0 - beta_two) * gradient * gradient
    update = new_one / bias_one / (jnp.sqrt(new_two / bias_two) + adam_floor)
    new_master = master - step_size * (update + weight_decay * master)
    return (new_master, new_one, new_two)


def exchange(x, bit, replica_count):
    return lax.ppermute(x, "dp", [(i, i ^ (1 << bit)) for i in range(replica_count)])


def partial_sum(block, first_row, rows, own, core, later):
    columns = pl.ds(pl.multiple_of(block * TILE, TILE), TILE)
    total = own[block >> 1, pl.ds(first_row, rows)].astype(jnp.float32)
    total = total + core[0, pl.ds(first_row, rows), columns].astype(jnp.float32)
    for step, received in enumerate(later):
        total = total + received[block >> (step + 2)].astype(jnp.float32)
    return total


def keeping_kernel(gradients, out, arrived):
    core = lax.axis_index("dp") & 1
    copies = []
    for q in range(out.shape[0]):
        columns = pl.ds(pl.multiple_of((2 * q + core) * TILE, TILE), TILE)
        copy = pltpu.make_async_copy(gradients.at[0, :, columns], out.at[q], arrived.at[q])
        copy.start()
        copies.append(copy)
    for copy in copies:
        copy.wait()


def keeping(gradients, replica_count):
    count, row_count = replica_count // 2, gradients.shape[1]
    return pl.pallas_call(
        keeping_kernel,
        out_shape=jax.ShapeDtypeStruct((count, row_count, TILE), jnp.bfloat16),
        in_specs=[ANY],
        out_specs=VMEM,
        scratch_shapes=[pltpu.SemaphoreType.DMA((count,))],
        compiler_params=pltpu.CompilerParams(vmem_limit_bytes=16 * 2**20),
        cost_estimate=pl.CostEstimate(
            flops=0, bytes_accessed=4 * count * row_count * TILE, transcendentals=0
        ),
    )(gradients)


def sending_kernel(bit, first_row, own, core, *rest):
    later, out = rest[:-1], rest[-1]
    place = lax.axis_index("dp")
    low = place & ((1 << bit) - 1)
    other = (1 - ((place >> bit) & 1)) << bit
    for q in range(out.shape[0]):
        block = (q << (bit + 1)) | other | low
        out[q] = partial_sum(block, first_row, out.shape[1], own, core, later).astype(out.dtype)


def sending(bit, first_row, rows, replica_count, own, core, later):
    shape = (replica_count >> (bit + 1), rows, TILE)
    return pl.pallas_call(
        functools.partial(sending_kernel, bit, first_row),
        out_shape=jax.ShapeDtypeStruct(shape, jnp.bfloat16),
        in_specs=[VMEM] * (2 + len(later)),
        out_specs=VMEM,
        compiler_params=pltpu.CompilerParams(vmem_limit_bytes=16 * 2**20),
        cost_estimate=pl.CostEstimate(
            flops=3 * shape[0] * rows * TILE, bytes_accessed=6 * shape[0] * rows * TILE, transcendentals=0
        ),
    )(own, core, *later)


def step_kernel(
    steps, replica_count, own, core, *rest
):
    later = rest[: steps * CHUNKS]
    master, one, two, synced, record, chooser = rest[steps * CHUNKS : steps * CHUNKS + 6]
    new_master, new_one, new_two, column_max, outgoing, clipped = rest[steps * CHUNKS + 6 :]
    place = lax.axis_index("dp")
    row_count = master.shape[0]
    rows = row_count // CHUNKS
    piece = TILE // 2
    for r in range(row_count // piece):
        at = pl.ds(r * piece, piece)
        columns = pl.ds(pl.multiple_of(place * TILE, TILE), TILE)
        total = own[place >> 1, at].astype(jnp.float32) + core[0, at, columns].astype(jnp.float32)
        chunk = r * piece // rows
        inner = pl.ds(r * piece - chunk * rows, piece)
        for step in range(steps):
            received = later[chunk * steps + step]
            total = total + received[place >> (step + 2), inner].astype(jnp.float32)
        a, b, c = adam_step(master[at], one[at], two[at], total / replica_count)
        new_master[at] = a
        new_one[at] = b
        new_two[at] = c
        delta = a - synced[at].astype(jnp.float32)
        tile = r * piece // TILE
        peak = jnp.max(jnp.abs(delta), axis=0, keepdims=True)
        if r * piece % TILE == 0:
            column_max[pl.ds(tile, 1)] = peak
        else:
            column_max[pl.ds(tile, 1)] = jnp.maximum(column_max[pl.ds(tile, 1)], peak)
        limit = record[0, tile]
        clipped[at] = jnp.clip(delta, -limit, limit).astype(jnp.bfloat16)
    outgoing[...] = jnp.dot(
        chooser[...], clipped[...], preferred_element_type=jnp.float32
    ).astype(jnp.bfloat16)


def body(
    gradients, master, moment_one, moment_two, synced, rollout, amax_record, row_table, expert_owner
):
    owner_count = lax.axis_size("fsdp")
    replica_count = lax.axis_size("dp")
    row_count, column_count = master.shape
    block_count = row_count // TILE
    per_owner = TILE // owner_count

    core = exchange(gradients, 0, replica_count)
    own = keeping(gradients, replica_count)
    rows = row_count // CHUNKS
    later = [[] for _ in range(CHUNKS)]
    steps = replica_count.bit_length() - 2
    for bit in range(1, steps + 1):
        for chunk in range(CHUNKS):
            out = sending(bit, chunk * rows, rows, replica_count, own, core, later[chunk])
            later[chunk].append(exchange(out, bit, replica_count))

    index = jnp.arange(TILE, dtype=jnp.int32)
    before = (row_table[None, :] < row_table[:, None]) | (
        (row_table[None, :] == row_table[:, None]) & (index[None, :] < index[:, None])
    )
    rank = jnp.sum(before.astype(jnp.int32), axis=1)
    blocks = jnp.arange(block_count, dtype=jnp.int32)
    experts = (lax.axis_index("fsdp") * block_count + blocks) * TILE // D
    shifts = expert_owner[experts]
    owner = (rank[None, :] // per_owner + shifts[:, None]) % owner_count
    slot = (owner * block_count + blocks[:, None]) * per_owner + rank[None, :] % per_owner
    chooser = (
        jnp.arange(row_count, dtype=jnp.int32)[:, None] == slot.reshape(1, row_count)
    ).astype(jnp.bfloat16)

    full = jax.ShapeDtypeStruct(master.shape, jnp.float32)
    new_master, new_one, new_two, column_max, outgoing = pl.pallas_call(
        functools.partial(step_kernel, steps, replica_count),
        out_shape=(
            full,
            full,
            full,
            jax.ShapeDtypeStruct((block_count, TILE), jnp.float32),
            jax.ShapeDtypeStruct(master.shape, jnp.bfloat16),
        ),
        in_specs=[VMEM] * (2 + steps * CHUNKS + 4) + [SMEM, VMEM],
        out_specs=(VMEM,) * 5,
        scratch_shapes=[pltpu.VMEM(master.shape, jnp.bfloat16)],
        compiler_params=pltpu.CompilerParams(vmem_limit_bytes=16 * 2**20),
    )(
        own,
        core,
        *[x for group in later for x in group],
        master,
        moment_one,
        moment_two,
        synced,
        amax_record.reshape(1, block_count),
        chooser,
    )
    new_amax = jnp.max(column_max, axis=1).reshape(block_count, 1)
    incoming = lax.all_to_all(
        outgoing.reshape(owner_count * block_count, per_owner, column_count),
        "fsdp",
        split_axis=0,
        concat_axis=0,
        tiled=True,
    ).reshape(row_count, column_count)
    new_rollout = (rollout.astype(jnp.float32) + incoming.astype(jnp.float32)).astype(jnp.bfloat16)
    return (new_master, new_one, new_two, new_amax, new_rollout)


def solution(mesh):
    return jax.shard_map(
        body,
        mesh=mesh,
        in_specs=(
            P("dp", "fsdp", None),
            P("fsdp", "dp"),
            P("fsdp", "dp"),
            P("fsdp", "dp"),
            P("fsdp", "dp"),
            P("fsdp", "dp"),
            P("fsdp", "dp"),
            P(),
            P(),
        ),
        out_specs=(
            P("fsdp", "dp"),
            P("fsdp", "dp"),
            P("fsdp", "dp"),
            P("fsdp", "dp"),
            P("fsdp", "dp"),
        ),
        check_vma=False,
    )
```

time: 99 us -> 90.1 us (0.910)
  the two profiles are of different devices: /device:TPU:8 before, /device:TPU:64 now
where the time goes in v2:
time: 90.1 us; the launch traced here: 89.7 us
  starting transfers between devices  51.9 us (58%)
  waiting for transfers between devices  30.9 us (34%)
  Pallas kernels  2.29 us (3%)
  local copies, waits for them, and re-layouts  2.09 us (2%)
  other arithmetic  1.66 us (2%)
    ppermute x7, starting transfers between devices, exchange(): lax.ppermute(x, 'dp', [(i, i ^ 1 << bit) for i in range(replica_count)])  31.8 us
    all_to_all x1, starting transfers between devices, body(): lax.all_to_all(outgoing.reshape(owner_count * block_count, per_owner, col...  20.1 us
    all_to_all x1, waiting for transfers between devices, body(): lax.all_to_all(outgoing.reshape(owner_count * block_count, per_owner, col...  18.7 us
    ppermute x7, waiting for transfers between devices, exchange(): lax.ppermute(x, 'dp', [(i, i ^ 1 << bit) for i in range(replica_count)])  12.1 us
  transfers between devices with their start and end apart: 8, of which 8 were waited for; matrix products, arithmetic and copies ran while one was open for 2% of the time, Pallas kernels for 1%

profile of v2, /device:TPU:64, one launch (start us, length us, event | category | flops | bytes accessed | tf_op | source)
XLA Modules:
  0.0 89.7 jit_solution(13189178217634763889)
XLA Ops:
  0.7 2.1 %collective-permute-start = (bf16[1,384,2048]{2,1,0:T(8,128)(2,1)}, bf16[1,384,2048]{2,1,0:T(8,128)(2,1)S(1)}, u32[]{:S(2)}, u32[]{:S(2)}) collective-permute-start(bf16[1,384,2048]{2,1,0:T(8,128)(2,1)} %gradients.1), channel_id=1, source_target_pairs={{0,64},{64,0},{128,192},{192,128},{256,320},{320,256},{384,448},{4... | collective-permute-start | bytes 4718600 | tf_op jit(solution)/shard_map/ppermute | solution.py:36
  2.7 1.4 %copy-done.1 = bf16[1,384,2048]{2,1,0:T(8,128)(2,1)S(1)} copy-done((bf16[1,384,2048]{2,1,0:T(8,128)(2,1)S(1)}, bf16[1,384,2048]{2,1,0:T(8,128)(2,1)}, u32[]{:S(2)}) %copy-start.1) | copy-done | bytes 1572888
  4.1 0.3 shard_map.128.own
  4.5 0.6 gather_fusion
  5.1 0.2 convert_reduce_fusion
  5.3 1.0 %collective-permute-done.core = bf16[1,384,2048]{2,1,0:T(8,128)(2,1)S(1)} collective-permute-done((bf16[1,384,2048]{2,1,0:T(8,128)(2,1)}, bf16[1,384,2048]{2,1,0:T(8,128)(2,1)S(1)}, u32[]{:S(2)}, u32[]{:S(2)}) %collective-permute-start) | collective-permute-done | bytes 1572896 | tf_op jit(solution)/shard_map/ppermute | solution.py:36
  6.4 14.2 %collective-permute-start.1 = (bf16[4,192,128]{2,1,0:T(8,128)(2,1)S(1)}, bf16[4,192,128]{2,1,0:T(8,128)(2,1)S(1)}, u32[]{:S(2)}, u32[]{:S(2)}) collective-permute-start(bf16[4,192,128]{2,1,0:T(8,128)(2,1)S(1)} %shard_map.129), channel_id=1, source_target_pairs={{0,128},{64,192},{128,0},{192,64},{256,384},{320,448},{384,256},{4... | collective-permute-start | bytes 589832 | tf_op jit(solution)/shard_map/ppermute | solution.py:36
  20.6 0.1 shard_map.132
  20.7 1.9 %collective-permute-start.4 = (bf16[4,192,128]{2,1,0:T(8,128)(2,1)S(1)}, bf16[4,192,128]{2,1,0:T(8,128)(2,1)S(1)}, u32[]{:S(2)}, u32[]{:S(2)}) collective-permute-start(bf16[4,192,128]{2,1,0:T(8,128)(2,1)S(1)} %shard_map.132), channel_id=1, source_target_pairs={{0,128},{64,192},{128,0},{192,64},{256,384},{320,448},{384,256},{4... | collective-permute-start | bytes 589832 | tf_op jit(solution)/shard_map/ppermute | solution.py:36
  22.6 3.6 %collective-permute-done.1.rest_0_ = bf16[4,192,128]{2,1,0:T(8,128)(2,1)S(1)} collective-permute-done((bf16[4,192,128]{2,1,0:T(8,128)(2,1)S(1)}, bf16[4,192,128]{2,1,0:T(8,128)(2,1)S(1)}, u32[]{:S(2)}, u32[]{:S(2)}) %collective-permute-start.1) | collective-permute-done | bytes 196640 | tf_op jit(solution)/shard_map/ppermute | solution.py:36
  26.3 1.9 %collective-permute-start.2 = (bf16[2,192,128]{2,1,0:T(8,128)(2,1)S(1)}, bf16[2,192,128]{2,1,0:T(8,128)(2,1)S(1)}, u32[]{:S(2)}, u32[]{:S(2)}) collective-permute-start(bf16[2,192,128]{2,1,0:T(8,128)(2,1)S(1)} %shard_map.130), channel_id=1, source_target_pairs={{0,256},{64,320},{128,384},{192,448},{256,0},{320,64},{384,128},{4... | collective-permute-start | bytes 294920 | tf_op jit(solution)/shard_map/ppermute | solution.py:36
  28.2 2.1 %collective-permute-done.4.rest_0_.rest_3_ = bf16[4,192,128]{2,1,0:T(8,128)(2,1)S(1)} collective-permute-done((bf16[4,192,128]{2,1,0:T(8,128)(2,1)S(1)}, bf16[4,192,128]{2,1,0:T(8,128)(2,1)S(1)}, u32[]{:S(2)}, u32[]{:S(2)}) %collective-permute-start.4) | collective-permute-done | bytes 196640 | tf_op jit(solution)/shard_map/ppermute | solution.py:36
  30.3 2.8 %collective-permute-start.5 = (bf16[2,192,128]{2,1,0:T(8,128)(2,1)S(1)}, bf16[2,192,128]{2,1,0:T(8,128)(2,1)S(1)}, u32[]{:S(2)}, u32[]{:S(2)}) collective-permute-start(bf16[2,192,128]{2,1,0:T(8,128)(2,1)S(1)} %shard_map.133), channel_id=1, source_target_pairs={{0,256},{64,320},{128,384},{192,448},{256,0},{320,64},{384,128},{4... | collective-permute-start | bytes 294920 | tf_op jit(solution)/shard_map/ppermute | solution.py:36
  33.1 0.1 fusion.8
  33.2 0.6 collective-permute-done.2.rest_1_
  33.9 2.9 %collective-permute-start.3 = (bf16[1,192,128]{2,1,0:T(8,128)(2,1)S(1)}, bf16[1,192,128]{2,1,0:T(8,128)(2,1)S(1)}, u32[]{:S(2)}, u32[]{:S(2)}) collective-permute-start(bf16[1,192,128]{2,1,0:T(8,128)(2,1)S(1)} %shard_map.131), channel_id=1, source_target_pairs={{0,512},{64,576},{128,640},{192,704},{256,768},{320,832},{384,896}... | collective-permute-start | bytes 147464 | tf_op jit(solution)/shard_map/ppermute | solution.py:36
  36.8 1.0 %collective-permute-done.5.rest_1_.rest_4_ = bf16[2,192,128]{2,1,0:T(8,128)(2,1)S(1)} collective-permute-done((bf16[2,192,128]{2,1,0:T(8,128)(2,1)S(1)}, bf16[2,192,128]{2,1,0:T(8,128)(2,1)S(1)}, u32[]{:S(2)}, u32[]{:S(2)}) %collective-permute-start.5) | collective-permute-done | bytes 98336 | tf_op jit(solution)/shard_map/ppermute | solution.py:36
  37.9 6.0 %collective-permute-start.6 = (bf16[1,192,128]{2,1,0:T(8,128)(2,1)S(1)}, bf16[1,192,128]{2,1,0:T(8,128)(2,1)S(1)}, u32[]{:S(2)}, u32[]{:S(2)}) collective-permute-start(bf16[1,192,128]{2,1,0:T(8,128)(2,1)S(1)} %shard_map.134), channel_id=1, source_target_pairs={{0,512},{64,576},{128,640},{192,704},{256,768},{320,832},{384,896}... | collective-permute-start | bytes 147464 | tf_op jit(solution)/shard_map/ppermute | solution.py:36
  44.0 3.8 %collective-permute-done.6.rest_5_ = bf16[1,192,128]{2,1,0:T(8,128)(2,1)S(1)} collective-permute-done((bf16[1,192,128]{2,1,0:T(8,128)(2,1)S(1)}, bf16[1,192,128]{2,1,0:T(8,128)(2,1)S(1)}, u32[]{:S(2)}, u32[]{:S(2)}) %collective-permute-start.6) | collective-permute-done | bytes 49184 | tf_op jit(solution)/shard_map/ppermute | solution.py:36
  47.8 1.7 %shard_map.135 = (f32[384,128]{1,0:T(8,128)}, f32[384,128]{1,0:T(8,128)}, f32[384,128]{1,0:T(8,128)}, f32[3,128]{1,0:T(4,128)S(1)}, bf16[384,128]{1,0:T(8,128)(2,1)}) custom-call(bf16[8,384,128]{2,1,0:T(8,128)(2,1)S(1)} %shard_map.128.own, bf16[1,384,2048]{2,1,0:T(8,128)(2,1)S(1)} %collective-permute-done.core, ...), custom_call_target="tpu_custom_call" | custom-call | tf_op jit(solution)/shard_map/pallas_call | solution.py:170
  49.5 20.1 %all-to-all-start = ((bf16[192,2,128]{2,1,0:T(2,128)(2,1)}), bf16[192,2,128]{2,1,0:T(2,128)(2,1)S(1)}, u32[]{:S(2)}, u32[]{:S(2)}) async-start(bf16[192,2,128]{2,1,0:T(2,128)(2,1)} %bitcast.6), calls=%async_computation | async-start | bytes 196608 | tf_op jit(solution)/shard_map/all_to_all | solution.py:195
  69.6 0.6 reduce_max.9
  70.2 18.7 %all-to-all-done = bf16[192,2,128]{2,1,0:T(2,128)(2,1)S(1)} async-done(((bf16[192,2,128]{2,1,0:T(2,128)(2,1)}), bf16[192,2,128]{2,1,0:T(2,128)(2,1)S(1)}, u32[]{:S(2)}, u32[]{:S(2)}) %all-to-all-start) | async-done | bytes 98336 | tf_op jit(solution)/shard_map/all_to_all | solution.py:195
  89.0 0.7 fusion.1
  (27 shorter events, 0.4 us)
Async XLA Ops:
  0.6 3.8 %copy-start = (s32[4]{0:T(128)S(1)}, s32[4]{0:T(128)}, u32[]{:S(2)}) copy-start(s32[4]{0:T(128)} %param.17) | copy-start | bytes 52
  0.6 4.5 %copy-start.8 = (s32[128]{0:T(128)S(1)}, s32[128]{0:T(128)}, u32[]{:S(2)}) copy-start(s32[128]{0:T(128)} %param.16) | copy-start | bytes 1540
  0.7 5.6 %collective-permute-start = (bf16[1,384,2048]{2,1,0:T(8,128)(2,1)}, bf16[1,384,2048]{2,1,0:T(8,128)(2,1)S(1)}, u32[]{:S(2)}, u32[]{:S(2)}) collective-permute-start(bf16[1,384,2048]{2,1,0:T(8,128)(2,1)} %gradients.1), channel_id=1, source_target_pairs={{0,64},{64,0},{128,192},{192,128},{256,320},{320,256},{384,448},{4... | collective-permute-start | bytes 4718600 | tf_op jit(solution)/shard_map/ppermute | solution.py:36
  2.7 1.4 %copy-start.1 = (bf16[1,384,2048]{2,1,0:T(8,128)(2,1)S(1)}, bf16[1,384,2048]{2,1,0:T(8,128)(2,1)}, u32[]{:S(2)}) copy-start(bf16[1,384,2048]{2,1,0:T(8,128)(2,1)} %gradients.1) | copy-start | bytes 4718596
  6.4 19.9 %collective-permute-start.1 = (bf16[4,192,128]{2,1,0:T(8,128)(2,1)S(1)}, bf16[4,192,128]{2,1,0:T(8,128)(2,1)S(1)}, u32[]{:S(2)}, u32[]{:S(2)}) collective-permute-start(bf16[4,192,128]{2,1,0:T(8,128)(2,1)S(1)} %shard_map.129), channel_id=1, source_target_pairs={{0,128},{64,192},{128,0},{192,64},{256,384},{320,448},{384,256},{4... | collective-permute-start | bytes 589832 | tf_op jit(solution)/shard_map/ppermute | solution.py:36
  20.7 9.6 %collective-permute-start.4 = (bf16[4,192,128]{2,1,0:T(8,128)(2,1)S(1)}, bf16[4,192,128]{2,1,0:T(8,128)(2,1)S(1)}, u32[]{:S(2)}, u32[]{:S(2)}) collective-permute-start(bf16[4,192,128]{2,1,0:T(8,128)(2,1)S(1)} %shard_map.132), channel_id=1, source_target_pairs={{0,128},{64,192},{128,0},{192,64},{256,384},{320,448},{384,256},{4... | collective-permute-start | bytes 589832 | tf_op jit(solution)/shard_map/ppermute | solution.py:36
  26.3 7.5 %collective-permute-start.2 = (bf16[2,192,128]{2,1,0:T(8,128)(2,1)S(1)}, bf16[2,192,128]{2,1,0:T(8,128)(2,1)S(1)}, u32[]{:S(2)}, u32[]{:S(2)}) collective-permute-start(bf16[2,192,128]{2,1,0:T(8,128)(2,1)S(1)} %shard_map.130), channel_id=1, source_target_pairs={{0,256},{64,320},{128,384},{192,448},{256,0},{320,64},{384,128},{4... | collective-permute-start | bytes 294920 | tf_op jit(solution)/shard_map/ppermute | solution.py:36
  30.3 7.5 %collective-permute-start.5 = (bf16[2,192,128]{2,1,0:T(8,128)(2,1)S(1)}, bf16[2,192,128]{2,1,0:T(8,128)(2,1)S(1)}, u32[]{:S(2)}, u32[]{:S(2)}) collective-permute-start(bf16[2,192,128]{2,1,0:T(8,128)(2,1)S(1)} %shard_map.133), channel_id=1, source_target_pairs={{0,256},{64,320},{128,384},{192,448},{256,0},{320,64},{384,128},{4... | collective-permute-start | bytes 294920 | tf_op jit(solution)/shard_map/ppermute | solution.py:36
  33.9 13.9 %copy-start.2 = (f32[384,128]{1,0:T(8,128)S(1)}, f32[384,128]{1,0:T(8,128)}, u32[]{:S(2)}) copy-start(f32[384,128]{1,0:T(8,128)} %rest_6_.1) | copy-start | bytes 589828
  33.9 13.9 %copy-start.3 = (f32[384,128]{1,0:T(8,128)S(1)}, f32[384,128]{1,0:T(8,128)}, u32[]{:S(2)}) copy-start(f32[384,128]{1,0:T(8,128)} %rest_7_.1) | copy-start | bytes 589828
  33.9 13.9 %copy-start.4 = (f32[384,128]{1,0:T(8,128)S(1)}, f32[384,128]{1,0:T(8,128)}, u32[]{:S(2)}) copy-start(f32[384,128]{1,0:T(8,128)} %rest_8_.1) | copy-start | bytes 589828
  33.9 13.9 %copy-start.5 = (bf16[384,128]{1,0:T(8,128)(2,1)S(1)}, bf16[384,128]{1,0:T(8,128)(2,1)}, u32[]{:S(2)}) copy-start(bf16[384,128]{1,0:T(8,128)(2,1)} %rest_9_.1) | copy-start | bytes 294916
  33.9 13.9 %copy-start.6 = (f32[3,1]{0,1:T(1,128)S(1)}, f32[3,1]{0,1:T(1,128)}, u32[]{:S(2)}) copy-start(f32[3,1]{0,1:T(1,128)} %param.15) | copy-start | bytes 40
  33.9 10.1 %collective-permute-start.3 = (bf16[1,192,128]{2,1,0:T(8,128)(2,1)S(1)}, bf16[1,192,128]{2,1,0:T(8,128)(2,1)S(1)}, u32[]{:S(2)}, u32[]{:S(2)}) collective-permute-start(bf16[1,192,128]{2,1,0:T(8,128)(2,1)S(1)} %shard_map.131), channel_id=1, source_target_pairs={{0,512},{64,576},{128,640},{192,704},{256,768},{320,832},{384,896}... | collective-permute-start | bytes 147464 | tf_op jit(solution)/shard_map/ppermute | solution.py:36
  37.9 9.9 %collective-permute-start.6 = (bf16[1,192,128]{2,1,0:T(8,128)(2,1)S(1)}, bf16[1,192,128]{2,1,0:T(8,128)(2,1)S(1)}, u32[]{:S(2)}, u32[]{:S(2)}) collective-permute-start(bf16[1,192,128]{2,1,0:T(8,128)(2,1)S(1)} %shard_map.134), channel_id=1, source_target_pairs={{0,512},{64,576},{128,640},{192,704},{256,768},{320,832},{384,896}... | collective-permute-start | bytes 147464 | tf_op jit(solution)/shard_map/ppermute | solution.py:36
  47.8 41.2 %copy-start.7 = (bf16[384,128]{1,0:T(8,128)(2,1)S(1)}, bf16[384,128]{1,0:T(8,128)(2,1)}, u32[]{:S(2)}) copy-start(bf16[384,128]{1,0:T(8,128)(2,1)} %param.14) | copy-start | bytes 294916
  49.5 39.5 %all-to-all-start = ((bf16[192,2,128]{2,1,0:T(2,128)(2,1)}), bf16[192,2,128]{2,1,0:T(2,128)(2,1)S(1)}, u32[]{:S(2)}, u32[]{:S(2)}) async-start(bf16[192,2,128]{2,1,0:T(2,128)(2,1)} %bitcast.6), calls=%async_computation | async-start | bytes 196608 | tf_op jit(solution)/shard_map/all_to_all | solution.py:195

commit v3 on v0

v3 whole, which is shorter than its diff:
```python
import functools

import jax
import jax.numpy as jnp
from jax import lax
from jax.experimental import pallas as pl
from jax.experimental.pallas import tpu as pltpu
from jax.sharding import PartitionSpec as P

D = 7168
TILE = 128
HALF = TILE // 2

beta_one = 0.9
beta_two = 0.95
bias_one = 1.0 - 0.9**10
bias_two = 1.0 - 0.95**10
step_size = 0.05
weight_decay = 0.1
adam_floor = 1e-08

VMEM = pl.BlockSpec(memory_space=pltpu.VMEM)
SMEM = pl.BlockSpec(memory_space=pltpu.SMEM)
ANY = pl.BlockSpec(memory_space=pl.ANY)
F32 = jnp.float32
BF16 = jnp.bfloat16


def adam_step(master, moment_one, moment_two, gradient):
    new_one = beta_one * moment_one + (1.0 - beta_one) * gradient
    new_two = beta_two * moment_two + (1.0 - beta_two) * gradient * gradient
    update = new_one / bias_one / (jnp.sqrt(new_two / bias_two) + adam_floor)
    new_master = master - step_size * (update + weight_decay * master)
    return (new_master, new_one, new_two)


def call(kernel, outs, ins, args, scratch=(), bytes_accessed=2**20):
    single = not isinstance(outs, (tuple, list))
    return pl.pallas_call(
        kernel,
        out_shape=outs,
        in_specs=ins,
        out_specs=VMEM if single else (VMEM,) * len(outs),
        scratch_shapes=list(scratch),
        compiler_params=pltpu.CompilerParams(vmem_limit_bytes=16 * 2**20),
        cost_estimate=pl.CostEstimate(
            flops=bytes_accessed, bytes_accessed=bytes_accessed, transcendentals=0
        ),
    )(*args)


def exchange(x, axis, distance, count):
    return lax.ppermute(x, axis, [(i, i ^ distance) for i in range(count)])


def ranks(across, down, axis):
    i = lax.broadcasted_iota(jnp.int32, (TILE, TILE), 1 - axis)
    j = lax.broadcasted_iota(jnp.int32, (TILE, TILE), axis)
    mine, other = (across, down) if axis == 0 else (down, across)
    before = (other < mine) | ((other == mine) & (j < i))
    return jnp.sum(before.astype(jnp.int32), axis=axis, keepdims=True)


def owners_of(rank, block, expert_owner, owner_count, block_count):
    per_owner = TILE // owner_count
    expert = (lax.axis_index("fsdp") * block_count + block) * TILE // D
    turned = rank // per_owner + expert_owner[expert]
    owner = jnp.where(turned >= owner_count, turned - owner_count, turned)
    half = owner_count // 2
    top = (owner >= half).astype(jnp.int32)
    inner = owner - top * half
    here = (lax.axis_index("fsdp") >= half).astype(jnp.int32)
    stays = (top == here).astype(jnp.int32)
    pair = rank - rank // per_owner * per_owner
    return inner, pair, stays, here


def picking_kernel(owner_count, across, down, expert_owner, picks):
    per_owner = TILE // owner_count
    block_count = picks.shape[0] // TILE
    rank = ranks(across[...], down[...], 0)
    place = lax.broadcasted_iota(jnp.int32, (HALF, TILE), 0)
    for block in range(block_count):
        inner, pair, stays, _ = owners_of(rank, block, expert_owner, owner_count, block_count)
        slot = inner * per_owner + pair + stays * HALF
        for chunk in range(2):
            at = (chunk * block_count + block) * HALF
            picks[pl.ds(at, HALF)] = (place + chunk * HALF == slot).astype(F32).astype(BF16)


def placing_kernel(owner_count, across, down, expert_owner, back_go, back_stay, pick_go, pack_stay):
    per_owner = TILE // owner_count
    row_count = back_go.shape[0]
    block_count = row_count // TILE
    chunk_rows = row_count // 2
    along = ranks(across[...], down[...], 0)
    upright = ranks(across[...], down[...], 1)
    lanes = lax.broadcasted_iota(jnp.int32, (TILE, chunk_rows), 1)
    sublanes = lax.broadcasted_iota(jnp.int32, (row_count, TILE), 0)
    for block in range(block_count):
        at = pl.ds(block * TILE, TILE)
        inner, pair, stays, _ = owners_of(upright, block, expert_owner, owner_count, block_count)
        slot = block * HALF + inner * per_owner + pair
        back_go[at] = (lanes == jnp.where(stays == 0, slot, -1)).astype(F32).astype(BF16)
        back_stay[at] = (lanes == jnp.where(stays == 1, slot, -1)).astype(F32).astype(BF16)
        inner, pair, stays, here = owners_of(along, block, expert_owner, owner_count, block_count)
        slot = block * HALF + inner * per_owner + pair
        pick_go[:, at] = (
            (sublanes[:chunk_rows] == jnp.where(stays == 0, slot, -1)).astype(F32).astype(BF16)
        )
        sent = ((inner * 2 + here) * block_count + block) * per_owner + pair
        pack_stay[:, at] = (sublanes == jnp.where(stays == 1, sent, -1)).astype(F32).astype(BF16)


def keeping_kernel(gradients, out, arrived):
    core = lax.axis_index("dp") & 1
    copies = []
    for q in range(out.shape[0]):
        columns = pl.ds(pl.multiple_of((2 * q + core) * TILE, TILE), TILE)
        copy = pltpu.make_async_copy(gradients.at[0, :, columns], out.at[q], arrived.at[q])
        copy.start()
        copies.append(copy)
    for copy in copies:
        copy.wait()


def first_kernel(sent, chunks, own, core, picks, out):
    place = lax.axis_index("dp")
    count, block_count = out.shape[0], own.shape[1] // TILE
    bit = (place >> 1) & 1
    wanted = (1 - bit) if sent else bit
    for r in range(block_count):
        at = pl.ds(r * TILE, TILE)
        sums = []
        for q in range(count):
            block = (q << 2) | (wanted << 1) | (place & 1)
            columns = pl.ds(pl.multiple_of(block * TILE, TILE), TILE)
            sums.append((own[block >> 1, at].astype(F32) + core[0, at, columns].astype(F32)).astype(BF16))
        joined = jnp.concatenate(sums, axis=1)
        for n, chunk in enumerate(chunks):
            pick = picks[pl.ds((chunk * block_count + r) * HALF, HALF)]
            moved = jnp.dot(pick, joined, preferred_element_type=F32).astype(BF16)
            for q in range(count):
                out[q, pl.ds((n * block_count + r) * HALF, HALF)] = moved[:, q * TILE : (q + 1) * TILE]


def sum_so_far(block, chunk, kept, later):
    rows = later[0].shape[1]
    total = kept[block >> 2, pl.ds(chunk * rows, rows)].astype(F32)
    for step, received in enumerate(later):
        total = total + received[block >> (step + 2)].astype(F32)
    return total


def sending_kernel(bit, chunk, kept, *rest):
    later, out = rest[:-1], rest[-1]
    place = lax.axis_index("dp")
    low = place & ((1 << bit) - 1)
    other = (1 - ((place >> bit) & 1)) << bit
    for q in range(out.shape[0]):
        block = (q << (bit + 1)) | other | low
        out[q] = sum_so_far(block, chunk, kept, later).astype(BF16)


def in_two(total, parts):
    high = total.astype(BF16)
    parts[:, :TILE] = high
    parts[:, TILE:] = (total - high.astype(F32)).astype(BF16)


def going_kernel(steps, replica_count, kept, *rest):
    later = rest[:steps]
    master, one, two, synced, record, back, pick, summed, outgoing, parts, clipped = rest[steps:]
    in_two(sum_so_far(lax.axis_index("dp"), 0, kept, later), parts)
    for tile in range(master.shape[0] // TILE):
        at = pl.ds(tile * TILE, TILE)
        pieces = jnp.dot(back[at], parts[...], preferred_element_type=F32)
        total = pieces[:, :TILE] + pieces[:, TILE:]
        summed[at] = total
        updated, _, _ = adam_step(master[at], one[at], two[at], total / replica_count)
        delta = updated - synced[at].astype(F32)
        limit = record[0, tile]
        clipped[at] = jnp.clip(delta, -limit, limit).astype(BF16)
    outgoing[...] = jnp.dot(pick[...], clipped[...], preferred_element_type=F32).astype(BF16)


def staying_kernel(steps, replica_count, kept, *rest):
    later = rest[:steps]
    master, one, two, synced, record, back, pack, summed = rest[steps : steps + 8]
    new_master, new_one, new_two, column_max, packed, parts, clipped = rest[steps + 8 :]
    in_two(sum_so_far(lax.axis_index("dp"), 1, kept, later), parts)
    for tile in range(master.shape[0] // TILE):
        at = pl.ds(tile * TILE, TILE)
        pieces = jnp.dot(back[at], parts[...], preferred_element_type=F32)
        total = summed[at] + (pieces[:, :TILE] + pieces[:, TILE:])
        a, b, c = adam_step(master[at], one[at], two[at], total / replica_count)
        new_master[at] = a
        new_one[at] = b
        new_two[at] = c
        delta = a - synced[at].astype(F32)
        column_max[pl.ds(tile, 1)] = jnp.max(jnp.abs(delta), axis=0, keepdims=True)
        limit = record[0, tile]
        clipped[at] = jnp.clip(delta, -limit, limit).astype(BF16)
    packed[...] = jnp.dot(pack[...], clipped[...], preferred_element_type=F32).astype(BF16)


def packing_kernel(owner_count, arrived, staying, out):
    per_owner = TILE // owner_count
    half = owner_count // 2
    row_count, chunk_rows = out.shape[0], arrived.shape[0]
    block_count = row_count // TILE
    there = 1 - (lax.axis_index("fsdp") >= half).astype(jnp.int32)
    row = lax.broadcasted_iota(jnp.int32, (1, chunk_rows), 1)
    block = row // HALF
    inner = (row - block * HALF) // per_owner
    pair = row - row // per_owner * per_owner
    sent = ((inner * 2 + there) * block_count + block) * per_owner + pair
    pack = (lax.broadcasted_iota(jnp.int32, (row_count, chunk_rows), 0) == sent).astype(F32).astype(BF16)
    moved = jnp.dot(pack, arrived[...], preferred_element_type=F32)
    out[...] = (moved + staying[...].astype(F32)).astype(BF16)


def adding_kernel(owner_count, incoming, rollout, out):
    group = rollout.shape[0] // owner_count
    half = owner_count // 2
    row_count = rollout.shape[0]
    row = lax.broadcasted_iota(jnp.int32, (1, row_count), 1)
    source = row // group
    wanted = ((source & 1) * half + (source >> 1)) * group + (row - source * group)
    order = (lax.broadcasted_iota(jnp.int32, (row_count, row_count), 0) == wanted).astype(F32).astype(BF16)
    moved = jnp.dot(order, incoming[...], preferred_element_type=F32)
    out[...] = (rollout[...].astype(F32) + moved).astype(BF16)


def body(
    gradients, master, moment_one, moment_two, synced, rollout, amax_record, row_table, expert_owner
):
    owner_count = lax.axis_size("fsdp")
    replica_count = lax.axis_size("dp")
    row_count, column_count = master.shape
    block_count = row_count // TILE
    rows = row_count // 2
    half = owner_count // 2

    def shape(*dims, dtype=BF16):
        return jax.ShapeDtypeStruct(dims, dtype)

    core = exchange(gradients, "dp", 1, replica_count)
    own = call(
        keeping_kernel,
        shape(replica_count // 2, row_count, TILE),
        [ANY],
        [gradients],
        [pltpu.SemaphoreType.DMA((replica_count // 2,))],
    )
    table = [row_table.reshape(1, TILE), row_table.reshape(TILE, 1), expert_owner]
    table_specs = [VMEM, VMEM, SMEM]
    picks = call(
        functools.partial(picking_kernel, owner_count), shape(row_count, TILE), table_specs, table
    )

    later = [[], []]
    steps = replica_count.bit_length() - 2
    for chunk in range(2):
        out = call(
            functools.partial(first_kernel, True, (chunk,)),
            shape(replica_count // 4, rows, TILE),
            [VMEM] * 3,
            [own, core, picks],
        )
        later[chunk].append(exchange(out, "dp", 2, replica_count))
    kept = call(
        functools.partial(first_kernel, False, (0, 1)),
        shape(replica_count // 4, row_count, TILE),
        [VMEM] * 3,
        [own, core, picks],
    )
    back_go, back_stay, pick_go, pack_stay = call(
        functools.partial(placing_kernel, owner_count),
        (
            shape(row_count, rows),
            shape(row_count, rows),
            shape(rows, row_count),
            shape(row_count, row_count),
        ),
        table_specs,
        table,
    )
    for bit in range(2, steps + 1):
        for chunk in range(2):
            out = call(
                functools.partial(sending_kernel, bit, chunk),
                shape(replica_count >> (bit + 1), rows, TILE),
                [VMEM] * (1 + len(later[chunk])),
                [kept, *later[chunk]],
            )
            later[chunk].append(exchange(out, "dp", 1 << bit, replica_count))

    state = [master, moment_one, moment_two, synced, amax_record.reshape(1, block_count)]
    state_specs = [VMEM] * 4 + [SMEM]
    scratch = [pltpu.VMEM((rows, 2 * TILE), BF16), pltpu.VMEM((row_count, TILE), BF16)]
    summed, outgoing = call(
        functools.partial(going_kernel, steps, replica_count),
        (shape(row_count, TILE, dtype=F32), shape(rows, TILE)),
        [VMEM] * (1 + steps) + state_specs + [VMEM] * 2,
        [kept, *later[0], *state, back_go, pick_go],
        scratch,
    )
    arrived = exchange(outgoing, "fsdp", half, owner_count)
    full = shape(row_count, TILE, dtype=F32)
    new_master, new_one, new_two, column_max, packed = call(
        functools.partial(staying_kernel, steps, replica_count),
        (full, full, full, shape(block_count, TILE, dtype=F32), shape(row_count, TILE)),
        [VMEM] * (1 + steps) + state_specs + [VMEM] * 3,
        [kept, *later[1], *state, back_stay, pack_stay, summed],
        scratch,
    )
    new_amax = jnp.max(column_max, axis=1).reshape(block_count, 1)
    packed = call(
        functools.partial(packing_kernel, owner_count),
        shape(row_count, TILE),
        [VMEM] * 2,
        [arrived, packed],
    )
    incoming = lax.all_to_all(
        packed.reshape(row_count // 2, 2, TILE),
        "fsdp",
        split_axis=0,
        concat_axis=0,
        axis_index_groups=[list(range(half)), list(range(half, owner_count))],
        tiled=True,
    ).reshape(row_count, TILE)
    new_rollout = call(
        functools.partial(adding_kernel, owner_count),
        shape(row_count, TILE),
        [VMEM] * 2,
        [incoming, rollout],
    )
    return (new_master, new_one, new_two, new_amax, new_rollout)


def solution(mesh):
    return jax.shard_map(
        body,
        mesh=mesh,
        in_specs=(
            P("dp", "fsdp", None),
            P("fsdp", "dp"),
            P("fsdp", "dp"),
            P("fsdp", "dp"),
            P("fsdp", "dp"),
            P("fsdp", "dp"),
            P("fsdp", "dp"),
            P(),
            P(),
        ),
        out_specs=(
            P("fsdp", "dp"),
            P("fsdp", "dp"),
            P("fsdp", "dp"),
            P("fsdp", "dp"),
            P("fsdp", "dp"),
        ),
        check_vma=False,
    )
```

time: 177 us -> 80.5 us (0.45)
  waiting for transfers between devices: 103 us -> 13.3 us
  starting transfers between devices: 41.5 us -> 55.3 us
  between operations: 14.2 us -> 0.93 us
  local copies, waits for them, and re-layouts: 13.1 us -> 2.21 us
  Pallas kernels: 0 us -> 7.73 us
  other arithmetic: 5.24 us -> 0.63 us
    unnamed x2 -> x0, waiting for transfers between devices: 85 us -> none
    ppermute x0 -> x8, starting transfers between devices: none -> 45.1 us  [exchange(): return lax.ppermute(x, axis, [(i, i ^ distance) for i in range(count)])]
    all_to_all x2 -> x1, starting transfers between devices: 41.5 us -> 10.2 us  [body(): lax.all_to_all(packed.reshape(row_count // 2, 2, TILE), 'fsdp', split_axi...]
    all_to_all x2 -> x1, waiting for transfers between devices: 17.6 us -> 8.65 us  [body(): lax.all_to_all(packed.reshape(row_count // 2, 2, TILE), 'fsdp', split_axi...]
    pallas_call x0 -> x14, Pallas kernels: none -> 7.73 us  [call(): pl.pallas_call(kernel, out_shape=outs, in_specs=ins, out_specs=VMEM if si...]
    gather x5 -> x0, local copies, waits for them, and re-layouts: 6.65 us -> none  [the longest x2 3.19 us: body(): code_values[jnp.arange(block_count, dtype=jnp.int32)[:, None, None], chosen]]
    ppermute x0 -> x8, waiting for transfers between devices: none -> 4.68 us  [exchange(): return lax.ppermute(x, axis, [(i, i ^ distance) for i in range(count)])]
    unnamed x18, local copies, waits for them, and re-layouts: 4.27 us -> 1.45 us
  transfers between devices with their start and end apart: 3 -> 9, of which waited for: 2 -> 5; matrix products, arithmetic and copies ran while one was open for 8% -> 2% of each run, Pallas kernels for 0% -> 7%
where the time goes in v3:
time: 80.5 us; the launch traced here: 80.1 us
  starting transfers between devices  55.3 us (69%)
  waiting for transfers between devices  13.3 us (17%)
  Pallas kernels  7.73 us (10%)
  local copies, waits for them, and re-layouts  2.21 us (3%)
  between operations  0.93 us (1%)
    ppermute x8, starting transfers between devices, exchange(): return lax.ppermute(x, axis, [(i, i ^ distance) for i in range(count)])  45.1 us
    all_to_all x1, starting transfers between devices, body(): lax.all_to_all(packed.reshape(row_count // 2, 2, TILE), 'fsdp', split_axi...  10.2 us
    all_to_all x1, waiting for transfers between devices, body(): lax.all_to_all(packed.reshape(row_count // 2, 2, TILE), 'fsdp', split_axi...  8.65 us
    pallas_call x14, Pallas kernels, call(): pl.pallas_call(kernel, out_shape=outs, in_specs=ins, out_specs=VMEM if si...  7.73 us
    ppermute x8, waiting for transfers between devices, exchange(): return lax.ppermute(x, axis, [(i, i ^ distance) for i in range(count)])  4.68 us
  transfers between devices with their start and end apart: 9, of which 5 were waited for; matrix products, arithmetic and copies ran while one was open for 2% of the time, Pallas kernels for 7%

profile of v3, /device:TPU:8, one launch (start us, length us, event | category | flops | bytes accessed | tf_op | source)
XLA Modules:
  0.0 80.1 jit_solution(5684737219770599287)
XLA Ops:
  0.7 2.1 %collective-permute-start = (bf16[1,384,2048]{2,1,0:T(8,128)(2,1)}, bf16[1,384,2048]{2,1,0:T(8,128)(2,1)S(1)}, u32[]{:S(2)}, u32[]{:S(2)}) collective-permute-start(bf16[1,384,2048]{2,1,0:T(8,128)(2,1)} %gradients.1), channel_id=1, source_target_pairs={{0,64},{64,0},{128,192},{192,128},{256,320},{320,256},{384,448},{4... | collective-permute-start | bytes 4718600 | tf_op jit(solution)/shard_map/ppermute | solution.py:53
  2.7 0.8 copy.14.down
  3.5 1.4 %copy-done = bf16[1,384,2048]{2,1,0:T(8,128)(2,1)S(1)} copy-done((bf16[1,384,2048]{2,1,0:T(8,128)(2,1)S(1)}, bf16[1,384,2048]{2,1,0:T(8,128)(2,1)}, u32[]{:S(2)}) %copy-start) | copy-done | bytes 1572888
  5.2 0.7 shard_map.129.picks
  5.9 0.4 collective-permute-done.core
  6.6 4.3 %collective-permute-start.4 = (bf16[4,192,128]{2,1,0:T(8,128)(2,1)S(1)}, bf16[4,192,128]{2,1,0:T(8,128)(2,1)S(1)}, u32[]{:S(2)}, u32[]{:S(2)}) collective-permute-start(bf16[4,192,128]{2,1,0:T(8,128)(2,1)S(1)} %shard_map.135), channel_id=1, source_target_pairs={{0,128},{64,192},{128,0},{192,64},{256,384},{320,448},{384,256},{4... | collective-permute-start | bytes 589832 | tf_op jit(solution)/shard_map/ppermute | solution.py:53
  11.2 1.9 %collective-permute-start.1 = (bf16[4,192,128]{2,1,0:T(8,128)(2,1)S(1)}, bf16[4,192,128]{2,1,0:T(8,128)(2,1)S(1)}, u32[]{:S(2)}, u32[]{:S(2)}) collective-permute-start(bf16[4,192,128]{2,1,0:T(8,128)(2,1)S(1)} %shard_map.131), channel_id=1, source_target_pairs={{0,128},{64,192},{128,0},{192,64},{256,384},{320,448},{384,256},{4... | collective-permute-start | bytes 589832 | tf_op jit(solution)/shard_map/ppermute | solution.py:53
  13.1 0.3 shard_map.130.kept
  13.5 3.1 %collective-permute-done.4.rest_0_ = bf16[4,192,128]{2,1,0:T(8,128)(2,1)S(1)} collective-permute-done((bf16[4,192,128]{2,1,0:T(8,128)(2,1)S(1)}, bf16[4,192,128]{2,1,0:T(8,128)(2,1)S(1)}, u32[]{:S(2)}, u32[]{:S(2)}) %collective-permute-start.4) | collective-permute-done | bytes 196640 | tf_op jit(solution)/shard_map/ppermute | solution.py:53
  16.6 6.1 %collective-permute-start.5 = (bf16[2,192,128]{2,1,0:T(8,128)(2,1)S(1)}, bf16[2,192,128]{2,1,0:T(8,128)(2,1)S(1)}, u32[]{:S(2)}, u32[]{:S(2)}) collective-permute-start(bf16[2,192,128]{2,1,0:T(8,128)(2,1)S(1)} %shard_map.136), channel_id=1, source_target_pairs={{0,256},{64,320},{128,384},{192,448},{256,0},{320,64},{384,128},{4... | collective-permute-start | bytes 294920 | tf_op jit(solution)/shard_map/ppermute | solution.py:53
  22.7 4.0 %collective-permute-start.2 = (bf16[2,192,128]{2,1,0:T(8,128)(2,1)S(1)}, bf16[2,192,128]{2,1,0:T(8,128)(2,1)S(1)}, u32[]{:S(2)}, u32[]{:S(2)}) collective-permute-start(bf16[2,192,128]{2,1,0:T(8,128)(2,1)S(1)} %shard_map.132), channel_id=1, source_target_pairs={{0,256},{64,320},{128,384},{192,448},{256,0},{320,64},{384,128},{4... | collective-permute-start | bytes 294920 | tf_op jit(solution)/shard_map/ppermute | solution.py:53
  26.7 0.3 collective-permute-done.5.rest_1_
  27.1 10.9 %collective-permute-start.6 = (bf16[1,192,128]{2,1,0:T(8,128)(2,1)S(1)}, bf16[1,192,128]{2,1,0:T(8,128)(2,1)S(1)}, u32[]{:S(2)}, u32[]{:S(2)}) collective-permute-start(bf16[1,192,128]{2,1,0:T(8,128)(2,1)S(1)} %shard_map.137), channel_id=1, source_target_pairs={{0,512},{64,576},{128,640},{192,704},{256,768},{320,832},{384,896}... | collective-permute-start | bytes 147464 | tf_op jit(solution)/shard_map/ppermute | solution.py:53
  38.0 1.0 %shard_map.134 = (bf16[384,192]{1,0:T(8,128)(2,1)S(1)}, bf16[384,192]{1,0:T(8,128)(2,1)S(1)}, bf16[192,384]{1,0:T(8,128)(2,1)S(1)}, bf16[384,384]{1,0:T(8,128)(2,1)S(1)}) custom-call(s32[1,128]{1,0:T(1,128)S(1)} %bitcast.9, s32[128,1]{1,0:T(8,128)S(1)} %copy.14.down, s32[4]{0:T(128)S(1)} %copy-done.7), custom_call_target="tpu_custom_call" | custom-call | flops 1048576 | bytes 1048576 | tf_op jit(solution)/shard_map/pallas_call | solution.py:39
  39.1 3.7 %collective-permute-start.3 = (bf16[1,192,128]{2,1,0:T(8,128)(2,1)S(1)}, bf16[1,192,128]{2,1,0:T(8,128)(2,1)S(1)}, u32[]{:S(2)}, u32[]{:S(2)}) collective-permute-start(bf16[1,192,128]{2,1,0:T(8,128)(2,1)S(1)} %shard_map.133), channel_id=1, source_target_pairs={{0,512},{64,576},{128,640},{192,704},{256,768},{320,832},{384,896}... | collective-permute-start | bytes 147464 | tf_op jit(solution)/shard_map/ppermute | solution.py:53
  42.9 1.1 %shard_map.138 = (f32[384,128]{1,0:T(8,128)S(1)}, bf16[192,128]{1,0:T(8,128)(2,1)S(1)}) custom-call(bf16[4,384,128]{2,1,0:T(8,128)(2,1)S(1)} %shard_map.130.kept, bf16[4,192,128]{2,1,0:T(8,128)(2,1)S(1)} %collective-permute-done.4.rest_0_, bf16[2,192,128]{2,1,0:T(8,128)(2,1)S(1)} %collective-permute-done.5.rest_1_, ...), custom_call_target="tpu_custom_call" | custom-call | flops 1048576 | bytes 1048576 | tf_op jit(solution)/shard_map/pallas_call | solution.py:39
  44.0 12.1 %collective-permute-start.7 = (bf16[192,128]{1,0:T(8,128)(2,1)S(1)}, bf16[192,128]{1,0:T(8,128)(2,1)S(1)}, u32[]{:S(2)}, u32[]{:S(2)}) collective-permute-start(bf16[192,128]{1,0:T(8,128)(2,1)S(1)} %get-tuple-element.25), channel_id=1, source_target_pairs={{0,32},{1,33},{2,34},{3,35},{4,36},{5,37},{6,38},{7,39},{8,40},{9,... | collective-permute-start | bytes 147464 | tf_op jit(solution)/shard_map/ppermute | solution.py:53
  56.2 1.8 %shard_map.139 = (f32[384,128]{1,0:T(8,128)}, f32[384,128]{1,0:T(8,128)}, f32[384,128]{1,0:T(8,128)}, f32[3,128]{1,0:T(4,128)S(1)}, bf16[384,128]{1,0:T(8,128)(2,1)S(1)}) custom-call(bf16[4,384,128]{2,1,0:T(8,128)(2,1)S(1)} %shard_map.130.kept, bf16[4,192,128]{2,1,0:T(8,128)(2,1)S(1)} %collective-permute-done.1.rest_0_, ...), custom_call_target="tpu_custom_call" | custom-call | flops 1048576 | bytes 1048576 | tf_op jit(solution)/shard_map/pallas_call | solution.py:39
  58.0 0.9 %collective-permute-done.7.arrived = bf16[192,128]{1,0:T(8,128)(2,1)S(1)} collective-permute-done((bf16[192,128]{1,0:T(8,128)(2,1)S(1)}, bf16[192,128]{1,0:T(8,128)(2,1)S(1)}, u32[]{:S(2)}, u32[]{:S(2)}) %collective-permute-start.7) | collective-permute-done | bytes 49184 | tf_op jit(solution)/shard_map/ppermute | solution.py:53
  58.9 0.8 %shard_map.140 = bf16[384,128]{1,0:T(8,128)(2,1)} custom-call(bf16[192,128]{1,0:T(8,128)(2,1)S(1)} %collective-permute-done.7.arrived, bf16[384,128]{1,0:T(8,128)(2,1)S(1)} %get-tuple-element.26.staying), custom_call_target="tpu_custom_call" | custom-call | flops 1048576 | bytes 1048576 | tf_op jit(solution)/shard_map/pallas_call | solution.py:39
  59.7 10.2 %all-to-all-start = ((bf16[192,2,128]{2,1,0:T(2,128)(2,1)}), bf16[192,2,128]{2,1,0:T(2,128)(2,1)S(1)}, u32[]{:S(2)}, u32[]{:S(2)}) async-start(bf16[192,2,128]{2,1,0:T(2,128)(2,1)} %bitcast.4), calls=%async_computation | async-start | bytes 196608 | tf_op jit(solution)/shard_map/all_to_all | solution.py:325
  69.9 0.6 reduce_max.9
  70.5 8.6 %all-to-all-done = bf16[192,2,128]{2,1,0:T(2,128)(2,1)S(1)} async-done(((bf16[192,2,128]{2,1,0:T(2,128)(2,1)}), bf16[192,2,128]{2,1,0:T(2,128)(2,1)S(1)}, u32[]{:S(2)}, u32[]{:S(2)}) %all-to-all-start) | async-done | bytes 98336 | tf_op jit(solution)/shard_map/all_to_all | solution.py:325
  79.2 0.9 %shard_map.141 = bf16[384,128]{1,0:T(8,128)(2,1)} custom-call(bf16[384,128]{1,0:T(8,128)(2,1)S(1)} %bitcast.6, bf16[384,128]{1,0:T(8,128)(2,1)S(1)} %copy-done.5), custom_call_target="tpu_custom_call" | custom-call | flops 1048576 | bytes 1048576 | tf_op jit(solution)/shard_map/pallas_call | solution.py:39
  (28 shorter events, 1.1 us)
Async XLA Ops:
  0.6 4.6 %copy-start.6 = (s32[128]{0:T(128)S(1)}, s32[128]{0:T(128)}, u32[]{:S(2)}) copy-start(s32[128]{0:T(128)} %param.16) | copy-start | bytes 1540
  0.6 4.6 %copy-start.7 = (s32[4]{0:T(128)S(1)}, s32[4]{0:T(128)}, u32[]{:S(2)}) copy-start(s32[4]{0:T(128)} %expert_owner.3) | copy-start | bytes 52
  0.7 5.6 %collective-permute-start = (bf16[1,384,2048]{2,1,0:T(8,128)(2,1)}, bf16[1,384,2048]{2,1,0:T(8,128)(2,1)S(1)}, u32[]{:S(2)}, u32[]{:S(2)}) collective-permute-start(bf16[1,384,2048]{2,1,0:T(8,128)(2,1)} %gradients.1), channel_id=1, source_target_pairs={{0,64},{64,0},{128,192},{192,128},{256,320},{320,256},{384,448},{4... | collective-permute-start | bytes 4718600 | tf_op jit(solution)/shard_map/ppermute | solution.py:53
  3.5 1.4 %copy-start = (bf16[1,384,2048]{2,1,0:T(8,128)(2,1)S(1)}, bf16[1,384,2048]{2,1,0:T(8,128)(2,1)}, u32[]{:S(2)}) copy-start(bf16[1,384,2048]{2,1,0:T(8,128)(2,1)} %gradients.1) | copy-start | bytes 4718596
  6.6 10.0 %collective-permute-start.4 = (bf16[4,192,128]{2,1,0:T(8,128)(2,1)S(1)}, bf16[4,192,128]{2,1,0:T(8,128)(2,1)S(1)}, u32[]{:S(2)}, u32[]{:S(2)}) collective-permute-start(bf16[4,192,128]{2,1,0:T(8,128)(2,1)S(1)} %shard_map.135), channel_id=1, source_target_pairs={{0,128},{64,192},{128,0},{192,64},{256,384},{320,448},{384,256},{4... | collective-permute-start | bytes 589832 | tf_op jit(solution)/shard_map/ppermute | solution.py:53
  11.2 11.5 %collective-permute-start.1 = (bf16[4,192,128]{2,1,0:T(8,128)(2,1)S(1)}, bf16[4,192,128]{2,1,0:T(8,128)(2,1)S(1)}, u32[]{:S(2)}, u32[]{:S(2)}) collective-permute-start(bf16[4,192,128]{2,1,0:T(8,128)(2,1)S(1)} %shard_map.131), channel_id=1, source_target_pairs={{0,128},{64,192},{128,0},{192,64},{256,384},{320,448},{384,256},{4... | collective-permute-start | bytes 589832 | tf_op jit(solution)/shard_map/ppermute | solution.py:53
  13.4 29.4 %copy-start.1 = (f32[384,128]{1,0:T(8,128)S(1)}, f32[384,128]{1,0:T(8,128)}, u32[]{:S(2)}) copy-start(f32[384,128]{1,0:T(8,128)} %rest_3_.3) | copy-start | bytes 589828
  13.4 29.4 %copy-start.2 = (f32[384,128]{1,0:T(8,128)S(1)}, f32[384,128]{1,0:T(8,128)}, u32[]{:S(2)}) copy-start(f32[384,128]{1,0:T(8,128)} %rest_4_.3) | copy-start | bytes 589828
  13.4 29.4 %copy-start.3 = (f32[384,128]{1,0:T(8,128)S(1)}, f32[384,128]{1,0:T(8,128)}, u32[]{:S(2)}) copy-start(f32[384,128]{1,0:T(8,128)} %rest_5_.3) | copy-start | bytes 589828
  13.5 29.4 %copy-start.4 = (bf16[384,128]{1,0:T(8,128)(2,1)S(1)}, bf16[384,128]{1,0:T(8,128)(2,1)}, u32[]{:S(2)}) copy-start(bf16[384,128]{1,0:T(8,128)(2,1)} %rest_6_.3) | copy-start | bytes 294916
  13.5 29.4 %copy-start.8 = (f32[3,1]{0,1:T(1,128)S(1)}, f32[3,1]{0,1:T(1,128)}, u32[]{:S(2)}) copy-start(f32[3,1]{0,1:T(1,128)} %param.15) | copy-start | bytes 40
  16.6 10.5 %collective-permute-start.5 = (bf16[2,192,128]{2,1,0:T(8,128)(2,1)S(1)}, bf16[2,192,128]{2,1,0:T(8,128)(2,1)S(1)}, u32[]{:S(2)}, u32[]{:S(2)}) collective-permute-start(bf16[2,192,128]{2,1,0:T(8,128)(2,1)S(1)} %shard_map.136), channel_id=1, source_target_pairs={{0,256},{64,320},{128,384},{192,448},{256,0},{320,64},{384,128},{4... | collective-permute-start | bytes 294920 | tf_op jit(solution)/shard_map/ppermute | solution.py:53
  22.7 16.3 %collective-permute-start.2 = (bf16[2,192,128]{2,1,0:T(8,128)(2,1)S(1)}, bf16[2,192,128]{2,1,0:T(8,128)(2,1)S(1)}, u32[]{:S(2)}, u32[]{:S(2)}) collective-permute-start(bf16[2,192,128]{2,1,0:T(8,128)(2,1)S(1)} %shard_map.132), channel_id=1, source_target_pairs={{0,256},{64,320},{128,384},{192,448},{256,0},{320,64},{384,128},{4... | collective-permute-start | bytes 294920 | tf_op jit(solution)/shard_map/ppermute | solution.py:53
  27.1 15.8 %collective-permute-start.6 = (bf16[1,192,128]{2,1,0:T(8,128)(2,1)S(1)}, bf16[1,192,128]{2,1,0:T(8,128)(2,1)S(1)}, u32[]{:S(2)}, u32[]{:S(2)}) collective-permute-start(bf16[1,192,128]{2,1,0:T(8,128)(2,1)S(1)} %shard_map.137), channel_id=1, source_target_pairs={{0,512},{64,576},{128,640},{192,704},{256,768},{320,832},{384,896}... | collective-permute-start | bytes 147464 | tf_op jit(solution)/shard_map/ppermute | solution.py:53
  39.1 17.1 %collective-permute-start.3 = (bf16[1,192,128]{2,1,0:T(8,128)(2,1)S(1)}, bf16[1,192,128]{2,1,0:T(8,128)(2,1)S(1)}, u32[]{:S(2)}, u32[]{:S(2)}) collective-permute-start(bf16[1,192,128]{2,1,0:T(8,128)(2,1)S(1)} %shard_map.133), channel_id=1, source_target_pairs={{0,512},{64,576},{128,640},{192,704},{256,768},{320,832},{384,896}... | collective-permute-start | bytes 147464 | tf_op jit(solution)/shard_map/ppermute | solution.py:53
  44.0 35.1 %copy-start.5 = (bf16[384,128]{1,0:T(8,128)(2,1)S(1)}, bf16[384,128]{1,0:T(8,128)(2,1)}, u32[]{:S(2)}) copy-start(bf16[384,128]{1,0:T(8,128)(2,1)} %rollout.1) | copy-start | bytes 294916
  44.0 14.8 %collective-permute-start.7 = (bf16[192,128]{1,0:T(8,128)(2,1)S(1)}, bf16[192,128]{1,0:T(8,128)(2,1)S(1)}, u32[]{:S(2)}, u32[]{:S(2)}) collective-permute-start(bf16[192,128]{1,0:T(8,128)(2,1)S(1)} %get-tuple-element.25), channel_id=1, source_target_pairs={{0,32},{1,33},{2,34},{3,35},{4,36},{5,37},{6,38},{7,39},{8,40},{9,... | collective-permute-start | bytes 147464 | tf_op jit(solution)/shard_map/ppermute | solution.py:53
  59.7 19.5 %all-to-all-start = ((bf16[192,2,128]{2,1,0:T(2,128)(2,1)}), bf16[192,2,128]{2,1,0:T(2,128)(2,1)S(1)}, u32[]{:S(2)}, u32[]{:S(2)}) async-start(bf16[192,2,128]{2,1,0:T(2,128)(2,1)} %bitcast.4), calls=%async_computation | async-start | bytes 196608 | tf_op jit(solution)/shard_map/all_to_all | solution.py:325

commit v4 on v3

--- a/solution.py
+++ b/solution.py
@@ -88,7 +88,20 @@
             picks[pl.ds(at, HALF)] = (place + chunk * HALF == slot).astype(F32).astype(BF16)
 
 
-def placing_kernel(owner_count, across, down, expert_owner, back_go, back_stay, pick_go, pack_stay):
+def placing_kernel(
+    owner_count,
+    across,
+    down,
+    expert_owner,
+    core,
+    back_go,
+    back_stay,
+    pick_go,
+    pack_stay,
+    pack_go,
+    order,
+):
+    del core
     per_owner = TILE // owner_count
     row_count = back_go.shape[0]
     block_count = row_count // TILE
@@ -111,6 +124,25 @@
         sent = ((inner * 2 + here) * block_count + block) * per_owner + pair
         pack_stay[:, at] = (sublanes == jnp.where(stays == 1, sent, -1)).astype(F32).astype(BF16)
 
+    half = owner_count // 2
+    there = 1 - (lax.axis_index("fsdp") >= half).astype(jnp.int32)
+    row = lax.broadcasted_iota(jnp.int32, (1, chunk_rows), 1)
+    block = row // HALF
+    inner = (row - block * HALF) // per_owner
+    pair = row - row // per_owner * per_owner
+    sent = ((inner * 2 + there) * block_count + block) * per_owner + pair
+    pack_go[...] = (
+        (lax.broadcasted_iota(jnp.int32, (row_count, chunk_rows), 0) == sent).astype(F32).astype(BF16)
+    )
+
+    group = block_count * per_owner
+    row = lax.broadcasted_iota(jnp.int32, (1, row_count), 1)
+    source = row // group
+    wanted = ((source & 1) * half + (source >> 1)) * group + (row - source * group)
+    order[...] = (
+        (lax.broadcasted_iota(jnp.int32, (row_count, row_count), 0) == wanted).astype(F32).astype(BF16)
+    )
+
 
 def keeping_kernel(gradients, out, arrived):
     core = lax.axis_index("dp") & 1
@@ -124,7 +156,8 @@
         copy.wait()
 
 
-def first_kernel(sent, chunks, own, core, picks, out):
+def first_kernel(sent, chunks, own, core, picks, *rest):
+    out = rest[-1]
     place = lax.axis_index("dp")
     count, block_count = out.shape[0], own.shape[1] // TILE
     bit = (place >> 1) & 1
@@ -204,31 +237,13 @@
     packed[...] = jnp.dot(pack[...], clipped[...], preferred_element_type=F32).astype(BF16)
 
 
-def packing_kernel(owner_count, arrived, staying, out):
-    per_owner = TILE // owner_count
-    half = owner_count // 2
-    row_count, chunk_rows = out.shape[0], arrived.shape[0]
-    block_count = row_count // TILE
-    there = 1 - (lax.axis_index("fsdp") >= half).astype(jnp.int32)
-    row = lax.broadcasted_iota(jnp.int32, (1, chunk_rows), 1)
-    block = row // HALF
-    inner = (row - block * HALF) // per_owner
-    pair = row - row // per_owner * per_owner
-    sent = ((inner * 2 + there) * block_count + block) * per_owner + pair
-    pack = (lax.broadcasted_iota(jnp.int32, (row_count, chunk_rows), 0) == sent).astype(F32).astype(BF16)
-    moved = jnp.dot(pack, arrived[...], preferred_element_type=F32)
+def packing_kernel(arrived, pack, staying, out):
+    moved = jnp.dot(pack[...], arrived[...], preferred_element_type=F32)
     out[...] = (moved + staying[...].astype(F32)).astype(BF16)
 
 
-def adding_kernel(owner_count, incoming, rollout, out):
-    group = rollout.shape[0] // owner_count
-    half = owner_count // 2
-    row_count = rollout.shape[0]
-    row = lax.broadcasted_iota(jnp.int32, (1, row_count), 1)
-    source = row // group
-    wanted = ((source & 1) * half + (source >> 1)) * group + (row - source * group)
-    order = (lax.broadcasted_iota(jnp.int32, (row_count, row_count), 0) == wanted).astype(F32).astype(BF16)
-    moved = jnp.dot(order, incoming[...], preferred_element_type=F32)
+def adding_kernel(incoming, order, rollout, out):
+    moved = jnp.dot(order[...], incoming[...], preferred_element_type=F32)
     out[...] = (rollout[...].astype(F32) + moved).astype(BF16)
 
 
@@ -261,31 +276,36 @@
 
     later = [[], []]
     steps = replica_count.bit_length() - 2
-    for chunk in range(2):
-        out = call(
-            functools.partial(first_kernel, True, (chunk,)),
-            shape(replica_count // 4, rows, TILE),
-            [VMEM] * 3,
-            [own, core, picks],
-        )
-        later[chunk].append(exchange(out, "dp", 2, replica_count))
+    sent = shape(replica_count // 4, rows, TILE)
+    summands = [own, core, picks]
+    first = call(functools.partial(first_kernel, True, (0,)), sent, [VMEM] * 3, summands)
+    later[0].append(exchange(first, "dp", 2, replica_count))
     kept = call(
         functools.partial(first_kernel, False, (0, 1)),
         shape(replica_count // 4, row_count, TILE),
         [VMEM] * 3,
-        [own, core, picks],
-    )
-    back_go, back_stay, pick_go, pack_stay = call(
+        summands,
+    )
+    back_go, back_stay, pick_go, pack_stay, pack_go, order = call(
         functools.partial(placing_kernel, owner_count),
         (
             shape(row_count, rows),
             shape(row_count, rows),
             shape(rows, row_count),
             shape(row_count, row_count),
+            shape(row_count, rows),
+            shape(row_count, row_count),
         ),
-        table_specs,
-        table,
-    )
+        [*table_specs, ANY],
+        [*table, core],
+    )
+    second = call(
+        functools.partial(first_kernel, True, (1,)),
+        sent,
+        [VMEM] * 3 + [ANY] * 2,
+        [*summands, kept, pick_go],
+    )
+    later[1].append(exchange(second, "dp", 2, replica_count))
     for bit in range(2, steps + 1):
         for chunk in range(2):
             out = call(
@@ -317,10 +337,10 @@
     )
     new_amax = jnp.max(column_max, axis=1).reshape(block_count, 1)
     packed = call(
-        functools.partial(packing_kernel, owner_count),
+        packing_kernel,
         shape(row_count, TILE),
-        [VMEM] * 2,
-        [arrived, packed],
+        [VMEM] * 3,
+        [arrived, pack_go, packed],
     )
     incoming = lax.all_to_all(
         packed.reshape(row_count // 2, 2, TILE),
@@ -331,10 +351,10 @@
         tiled=True,
     ).reshape(row_count, TILE)
     new_rollout = call(
-        functools.partial(adding_kernel, owner_count),
+        adding_kernel,
         shape(row_count, TILE),
-        [VMEM] * 2,
-        [incoming, rollout],
+        [VMEM] * 3,
+        [incoming, order, rollout],
     )
     return (new_master, new_one, new_two, new_amax, new_rollout)
 

time: 80.5 us -> 82.4 us (1.024)
  starting transfers between devices: 55.3 us -> 59.5 us
  waiting for transfers between devices: 13.3 us -> 10.8 us
    ppermute x8, starting transfers between devices: 45.1 us -> 48 us  [exchange(): return lax.ppermute(x, axis, [(i, i ^ distance) for i in range(count)])]
    ppermute x8, waiting for transfers between devices: 4.68 us -> 2.08 us  [exchange(): return lax.ppermute(x, axis, [(i, i ^ distance) for i in range(count)])]
    all_to_all x1, starting transfers between devices: 10.2 us -> 11.5 us  [body(): lax.all_to_all(packed.reshape(row_count // 2, 2, TILE), 'fsdp', split_axi...]
where the time goes in v4:
time: 82.4 us; the launch traced here: 82 us
  starting transfers between devices  59.5 us (72%)
  waiting for transfers between devices  10.8 us (13%)
  Pallas kernels  7.84 us (10%)
  local copies, waits for them, and re-layouts  2.21 us (3%)
  between operations  0.92 us (1%)
    ppermute x8, starting transfers between devices, exchange(): return lax.ppermute(x, axis, [(i, i ^ distance) for i in range(count)])  48 us
    all_to_all x1, starting transfers between devices, body(): lax.all_to_all(packed.reshape(row_count // 2, 2, TILE), 'fsdp', split_axi...  11.5 us
    all_to_all x1, waiting for transfers between devices, body(): lax.all_to_all(packed.reshape(row_count // 2, 2, TILE), 'fsdp', split_axi...  8.77 us
    pallas_call x14, Pallas kernels, call(): pl.pallas_call(kernel, out_shape=outs, in_specs=ins, out_specs=VMEM if si...  7.84 us
    ppermute x8, waiting for transfers between devices, exchange(): return lax.ppermute(x, axis, [(i, i ^ distance) for i in range(count)])  2.08 us
  transfers between devices with their start and end apart: 9, of which 5 were waited for; matrix products, arithmetic and copies ran while one was open for 2% of the time, Pallas kernels for 7%

profile of v4, /device:TPU:8, one launch (start us, length us, event | category | flops | bytes accessed | tf_op | source)
XLA Modules:
  0.0 82.0 jit_solution(15273250622906180548)
XLA Ops:
  0.7 2.1 %collective-permute-start = (bf16[1,384,2048]{2,1,0:T(8,128)(2,1)}, bf16[1,384,2048]{2,1,0:T(8,128)(2,1)S(1)}, u32[]{:S(2)}, u32[]{:S(2)}) collective-permute-start(bf16[1,384,2048]{2,1,0:T(8,128)(2,1)} %gradients.1), channel_id=1, source_target_pairs={{0,64},{64,0},{128,192},{192,128},{256,320},{320,256},{384,448},{4... | collective-permute-start | bytes 4718600 | tf_op jit(solution)/shard_map/ppermute | solution.py:53
  2.7 0.8 copy.14.down
  3.5 1.4 %copy-done = bf16[1,384,2048]{2,1,0:T(8,128)(2,1)S(1)} copy-done((bf16[1,384,2048]{2,1,0:T(8,128)(2,1)S(1)}, bf16[1,384,2048]{2,1,0:T(8,128)(2,1)}, u32[]{:S(2)}) %copy-start) | copy-done | bytes 1572888
  4.9 0.3 shard_map.128.own
  5.2 0.7 shard_map.129.picks
  5.9 0.4 collective-permute-done.core
  6.6 4.3 %collective-permute-start.4 = (bf16[4,192,128]{2,1,0:T(8,128)(2,1)S(1)}, bf16[4,192,128]{2,1,0:T(8,128)(2,1)S(1)}, u32[]{:S(2)}, u32[]{:S(2)}) collective-permute-start(bf16[4,192,128]{2,1,0:T(8,128)(2,1)S(1)} %shard_map.135), channel_id=1, source_target_pairs={{0,128},{64,192},{128,0},{192,64},{256,384},{320,448},{384,256},{4... | collective-permute-start | bytes 589832 | tf_op jit(solution)/shard_map/ppermute | solution.py:53
  10.9 0.3 shard_map.130.rest_0_.kept
  11.2 1.2 %shard_map.131 = (bf16[384,192]{1,0:T(8,128)(2,1)S(1)}, bf16[384,192]{1,0:T(8,128)(2,1)S(1)}, bf16[192,384]{1,0:T(8,128)(2,1)S(1)}, bf16[384,384]{1,0:T(8,128)(2...) custom-call(s32[1,128]{1,0:T(1,128)S(1)} %bitcast.9, s32[128,1]{1,0:T(8,128)S(1)} %copy.14.down, ...), custom_call_target="tpu_custom_call" | custom-call | flops 1048576 | bytes 1048576 | tf_op jit(solution)/shard_map/pallas_call | solution.py:39
  12.7 2.1 %collective-permute-start.1 = (bf16[4,192,128]{2,1,0:T(8,128)(2,1)S(1)}, bf16[4,192,128]{2,1,0:T(8,128)(2,1)S(1)}, u32[]{:S(2)}, u32[]{:S(2)}) collective-permute-start(bf16[4,192,128]{2,1,0:T(8,128)(2,1)S(1)} %shard_map.132), channel_id=1, source_target_pairs={{0,128},{64,192},{128,0},{192,64},{256,384},{320,448},{384,256},{4... | collective-permute-start | bytes 589832 | tf_op jit(solution)/shard_map/ppermute | solution.py:53
  14.8 1.2 %collective-permute-done.4.rest_0_ = bf16[4,192,128]{2,1,0:T(8,128)(2,1)S(1)} collective-permute-done((bf16[4,192,128]{2,1,0:T(8,128)(2,1)S(1)}, bf16[4,192,128]{2,1,0:T(8,128)(2,1)S(1)}, u32[]{:S(2)}, u32[]{:S(2)}) %collective-permute-start.4) | collective-permute-done | bytes 196640 | tf_op jit(solution)/shard_map/ppermute | solution.py:53
  16.1 6.1 %collective-permute-start.5 = (bf16[2,192,128]{2,1,0:T(8,128)(2,1)S(1)}, bf16[2,192,128]{2,1,0:T(8,128)(2,1)S(1)}, u32[]{:S(2)}, u32[]{:S(2)}) collective-permute-start(bf16[2,192,128]{2,1,0:T(8,128)(2,1)S(1)} %shard_map.136), channel_id=1, source_target_pairs={{0,256},{64,320},{128,384},{192,448},{256,0},{320,64},{384,128},{4... | collective-permute-start | bytes 294920 | tf_op jit(solution)/shard_map/ppermute | solution.py:53
  22.2 6.3 %collective-permute-start.2 = (bf16[2,192,128]{2,1,0:T(8,128)(2,1)S(1)}, bf16[2,192,128]{2,1,0:T(8,128)(2,1)S(1)}, u32[]{:S(2)}, u32[]{:S(2)}) collective-permute-start(bf16[2,192,128]{2,1,0:T(8,128)(2,1)S(1)} %shard_map.133), channel_id=1, source_target_pairs={{0,256},{64,320},{128,384},{192,448},{256,0},{320,64},{384,128},{4... | collective-permute-start | bytes 294920 | tf_op jit(solution)/shard_map/ppermute | solution.py:53
  28.7 10.9 %collective-permute-start.6 = (bf16[1,192,128]{2,1,0:T(8,128)(2,1)S(1)}, bf16[1,192,128]{2,1,0:T(8,128)(2,1)S(1)}, u32[]{:S(2)}, u32[]{:S(2)}) collective-permute-start(bf16[1,192,128]{2,1,0:T(8,128)(2,1)S(1)} %shard_map.137), channel_id=1, source_target_pairs={{0,512},{64,576},{128,640},{192,704},{256,768},{320,832},{384,896}... | collective-permute-start | bytes 147464 | tf_op jit(solution)/shard_map/ppermute | solution.py:53
  39.6 3.5 %collective-permute-start.3 = (bf16[1,192,128]{2,1,0:T(8,128)(2,1)S(1)}, bf16[1,192,128]{2,1,0:T(8,128)(2,1)S(1)}, u32[]{:S(2)}, u32[]{:S(2)}) collective-permute-start(bf16[1,192,128]{2,1,0:T(8,128)(2,1)S(1)} %shard_map.134), channel_id=1, source_target_pairs={{0,512},{64,576},{128,640},{192,704},{256,768},{320,832},{384,896}... | collective-permute-start | bytes 147464 | tf_op jit(solution)/shard_map/ppermute | solution.py:53
  43.2 1.1 %shard_map.138 = (f32[384,128]{1,0:T(8,128)S(1)}, bf16[192,128]{1,0:T(8,128)(2,1)S(1)}) custom-call(bf16[4,384,128]{2,1,0:T(8,128)(2,1)S(1)} %shard_map.130.rest_0_.kept, bf16[4,192,128]{2,1,0:T(8,128)(2,1)S(1)} %collective-permute-done.4.rest_0_, bf16[2,192,128]{2,1,0:T(8,128)(2,1)S(1)} %collective-permute-done.5.rest_1_, ...), custom_call_target="tpu_custom_call" | custom-call | flops 1048576 | bytes 1048576 | tf_op jit(solution)/shard_map/pallas_call | solution.py:39
  44.4 12.8 %collective-permute-start.7 = (bf16[192,128]{1,0:T(8,128)(2,1)S(1)}, bf16[192,128]{1,0:T(8,128)(2,1)S(1)}, u32[]{:S(2)}, u32[]{:S(2)}) collective-permute-start(bf16[192,128]{1,0:T(8,128)(2,1)S(1)} %get-tuple-element.27), channel_id=1, source_target_pairs={{0,32},{1,33},{2,34},{3,35},{4,36},{5,37},{6,38},{7,39},{8,40},{9,... | collective-permute-start | bytes 147464 | tf_op jit(solution)/shard_map/ppermute | solution.py:53
  57.2 1.8 %shard_map.139 = (f32[384,128]{1,0:T(8,128)}, f32[384,128]{1,0:T(8,128)}, f32[384,128]{1,0:T(8,128)}, f32[3,128]{1,0:T(4,128)S(1)}, bf16[384,128]{1,0:T(8,128)(2,1)S(1)}) custom-call(bf16[4,384,128]{2,1,0:T(8,128)(2,1)S(1)} %shard_map.130.rest_0_.kept, bf16[4,192,128]{2,1,0:T(8,128)(2,1)S(1)} %collective-permute-done.1.rest_0_, ...), custom_call_target="tpu_custom_call" | custom-call | flops 1048576 | bytes 1048576 | tf_op jit(solution)/shard_map/pallas_call | solution.py:39
  59.0 0.3 collective-permute-done.7.arrived
  59.3 0.8 %shard_map.140 = bf16[384,128]{1,0:T(8,128)(2,1)} custom-call(bf16[192,128]{1,0:T(8,128)(2,1)S(1)} %collective-permute-done.7.arrived, bf16[384,192]{1,0:T(8,128)(2,1)S(1)} %get-tuple-element.28.pack, bf16[384,128]{1,0:T(8,128)(2,1)S(1)} %get-tuple-element.29.staying), custom_call_target="tpu_custom_call" | custom-call | flops 1048576 | bytes 1048576 | tf_op jit(solution)/shard_map/pallas_call | solution.py:39
  60.2 11.5 %all-to-all-start = ((bf16[192,2,128]{2,1,0:T(2,128)(2,1)}), bf16[192,2,128]{2,1,0:T(2,128)(2,1)S(1)}, u32[]{:S(2)}, u32[]{:S(2)}) async-start(bf16[192,2,128]{2,1,0:T(2,128)(2,1)} %bitcast.4), calls=%async_computation | async-start | bytes 196608 | tf_op jit(solution)/shard_map/all_to_all | solution.py:345
  71.7 0.6 reduce_max.9
  72.3 8.8 %all-to-all-done = bf16[192,2,128]{2,1,0:T(2,128)(2,1)S(1)} async-done(((bf16[192,2,128]{2,1,0:T(2,128)(2,1)}), bf16[192,2,128]{2,1,0:T(2,128)(2,1)S(1)}, u32[]{:S(2)}, u32[]{:S(2)}) %all-to-all-start) | async-done | bytes 98336 | tf_op jit(solution)/shard_map/all_to_all | solution.py:345
  81.1 0.9 %shard_map.141 = bf16[384,128]{1,0:T(8,128)(2,1)} custom-call(bf16[384,128]{1,0:T(8,128)(2,1)S(1)} %bitcast.6, bf16[384,384]{1,0:T(8,128)(2,1)S(1)} %get-tuple-element.30.order, bf16[384,128]{1,0:T(8,128)(2,1)S(1)} %copy-done.5), custom_call_target="tpu_custom_call" | custom-call | flops 1048576 | bytes 1048576 | tf_op jit(solution)/shard_map/pallas_call | solution.py:39
  (28 shorter events, 0.9 us)
Async XLA Ops:
  0.6 4.6 %copy-start.6 = (s32[128]{0:T(128)S(1)}, s32[128]{0:T(128)}, u32[]{:S(2)}) copy-start(s32[128]{0:T(128)} %param.16) | copy-start | bytes 1540
  0.6 4.6 %copy-start.7 = (s32[4]{0:T(128)S(1)}, s32[4]{0:T(128)}, u32[]{:S(2)}) copy-start(s32[4]{0:T(128)} %expert_owner.3) | copy-start | bytes 52
  0.7 5.6 %collective-permute-start = (bf16[1,384,2048]{2,1,0:T(8,128)(2,1)}, bf16[1,384,2048]{2,1,0:T(8,128)(2,1)S(1)}, u32[]{:S(2)}, u32[]{:S(2)}) collective-permute-start(bf16[1,384,2048]{2,1,0:T(8,128)(2,1)} %gradients.1), channel_id=1, source_target_pairs={{0,64},{64,0},{128,192},{192,128},{256,320},{320,256},{384,448},{4... | collective-permute-start | bytes 4718600 | tf_op jit(solution)/shard_map/ppermute | solution.py:53
  3.5 1.4 %copy-start = (bf16[1,384,2048]{2,1,0:T(8,128)(2,1)S(1)}, bf16[1,384,2048]{2,1,0:T(8,128)(2,1)}, u32[]{:S(2)}) copy-start(bf16[1,384,2048]{2,1,0:T(8,128)(2,1)} %gradients.1) | copy-start | bytes 4718596
  6.6 9.5 %collective-permute-start.4 = (bf16[4,192,128]{2,1,0:T(8,128)(2,1)S(1)}, bf16[4,192,128]{2,1,0:T(8,128)(2,1)S(1)}, u32[]{:S(2)}, u32[]{:S(2)}) collective-permute-start(bf16[4,192,128]{2,1,0:T(8,128)(2,1)S(1)} %shard_map.135), channel_id=1, source_target_pairs={{0,128},{64,192},{128,0},{192,64},{256,384},{320,448},{384,256},{4... | collective-permute-start | bytes 589832 | tf_op jit(solution)/shard_map/ppermute | solution.py:53
  12.7 30.5 %copy-start.1 = (f32[384,128]{1,0:T(8,128)S(1)}, f32[384,128]{1,0:T(8,128)}, u32[]{:S(2)}) copy-start(f32[384,128]{1,0:T(8,128)} %rest_3_.3) | copy-start | bytes 589828
  12.7 30.5 %copy-start.2 = (f32[384,128]{1,0:T(8,128)S(1)}, f32[384,128]{1,0:T(8,128)}, u32[]{:S(2)}) copy-start(f32[384,128]{1,0:T(8,128)} %rest_4_.3) | copy-start | bytes 589828
  12.7 30.5 %copy-start.3 = (f32[384,128]{1,0:T(8,128)S(1)}, f32[384,128]{1,0:T(8,128)}, u32[]{:S(2)}) copy-start(f32[384,128]{1,0:T(8,128)} %rest_5_.3) | copy-start | bytes 589828
  12.7 30.5 %copy-start.4 = (bf16[384,128]{1,0:T(8,128)(2,1)S(1)}, bf16[384,128]{1,0:T(8,128)(2,1)}, u32[]{:S(2)}) copy-start(bf16[384,128]{1,0:T(8,128)(2,1)} %rest_6_.3) | copy-start | bytes 294916
  12.7 30.5 %copy-start.8 = (f32[3,1]{0,1:T(1,128)S(1)}, f32[3,1]{0,1:T(1,128)}, u32[]{:S(2)}) copy-start(f32[3,1]{0,1:T(1,128)} %param.15) | copy-start | bytes 40
  12.7 9.5 %collective-permute-start.1 = (bf16[4,192,128]{2,1,0:T(8,128)(2,1)S(1)}, bf16[4,192,128]{2,1,0:T(8,128)(2,1)S(1)}, u32[]{:S(2)}, u32[]{:S(2)}) collective-permute-start(bf16[4,192,128]{2,1,0:T(8,128)(2,1)S(1)} %shard_map.132), channel_id=1, source_target_pairs={{0,128},{64,192},{128,0},{192,64},{256,384},{320,448},{384,256},{4... | collective-permute-start | bytes 589832 | tf_op jit(solution)/shard_map/ppermute | solution.py:53
  16.1 12.5 %collective-permute-start.5 = (bf16[2,192,128]{2,1,0:T(8,128)(2,1)S(1)}, bf16[2,192,128]{2,1,0:T(8,128)(2,1)S(1)}, u32[]{:S(2)}, u32[]{:S(2)}) collective-permute-start(bf16[2,192,128]{2,1,0:T(8,128)(2,1)S(1)} %shard_map.136), channel_id=1, source_target_pairs={{0,256},{64,320},{128,384},{192,448},{256,0},{320,64},{384,128},{4... | collective-permute-start | bytes 294920 | tf_op jit(solution)/shard_map/ppermute | solution.py:53
  22.2 17.3 %collective-permute-start.2 = (bf16[2,192,128]{2,1,0:T(8,128)(2,1)S(1)}, bf16[2,192,128]{2,1,0:T(8,128)(2,1)S(1)}, u32[]{:S(2)}, u32[]{:S(2)}) collective-permute-start(bf16[2,192,128]{2,1,0:T(8,128)(2,1)S(1)} %shard_map.133), channel_id=1, source_target_pairs={{0,256},{64,320},{128,384},{192,448},{256,0},{320,64},{384,128},{4... | collective-permute-start | bytes 294920 | tf_op jit(solution)/shard_map/ppermute | solution.py:53
  28.7 14.5 %collective-permute-start.6 = (bf16[1,192,128]{2,1,0:T(8,128)(2,1)S(1)}, bf16[1,192,128]{2,1,0:T(8,128)(2,1)S(1)}, u32[]{:S(2)}, u32[]{:S(2)}) collective-permute-start(bf16[1,192,128]{2,1,0:T(8,128)(2,1)S(1)} %shard_map.137), channel_id=1, source_target_pairs={{0,512},{64,576},{128,640},{192,704},{256,768},{320,832},{384,896}... | collective-permute-start | bytes 147464 | tf_op jit(solution)/shard_map/ppermute | solution.py:53
  39.6 17.6 %collective-permute-start.3 = (bf16[1,192,128]{2,1,0:T(8,128)(2,1)S(1)}, bf16[1,192,128]{2,1,0:T(8,128)(2,1)S(1)}, u32[]{:S(2)}, u32[]{:S(2)}) collective-permute-start(bf16[1,192,128]{2,1,0:T(8,128)(2,1)S(1)} %shard_map.134), channel_id=1, source_target_pairs={{0,512},{64,576},{128,640},{192,704},{256,768},{320,832},{384,896}... | collective-permute-start | bytes 147464 | tf_op jit(solution)/shard_map/ppermute | solution.py:53
  44.4 36.7 %copy-start.5 = (bf16[384,128]{1,0:T(8,128)(2,1)S(1)}, bf16[384,128]{1,0:T(8,128)(2,1)}, u32[]{:S(2)}) copy-start(bf16[384,128]{1,0:T(8,128)(2,1)} %rollout.1) | copy-start | bytes 294916
  44.4 15.0 %collective-permute-start.7 = (bf16[192,128]{1,0:T(8,128)(2,1)S(1)}, bf16[192,128]{1,0:T(8,128)(2,1)S(1)}, u32[]{:S(2)}, u32[]{:S(2)}) collective-permute-start(bf16[192,128]{1,0:T(8,128)(2,1)S(1)} %get-tuple-element.27), channel_id=1, source_target_pairs={{0,32},{1,33},{2,34},{3,35},{4,36},{5,37},{6,38},{7,39},{8,40},{9,... | collective-permute-start | bytes 147464 | tf_op jit(solution)/shard_map/ppermute | solution.py:53
  60.2 20.9 %all-to-all-start = ((bf16[192,2,128]{2,1,0:T(2,128)(2,1)}), bf16[192,2,128]{2,1,0:T(2,128)(2,1)S(1)}, u32[]{:S(2)}, u32[]{:S(2)}) async-start(bf16[192,2,128]{2,1,0:T(2,128)(2,1)} %bitcast.4), calls=%async_computation | async-start | bytes 196608 | tf_op jit(solution)/shard_map/all_to_all | solution.py:345

commit v5 on v4

--- a/solution.py
+++ b/solution.py
@@ -53,9 +53,10 @@
     return lax.ppermute(x, axis, [(i, i ^ distance) for i in range(count)])
 
 
-def ranks(across, down, axis):
+def ranks(across, axis):
     i = lax.broadcasted_iota(jnp.int32, (TILE, TILE), 1 - axis)
     j = lax.broadcasted_iota(jnp.int32, (TILE, TILE), axis)
+    down = jnp.sum(jnp.where(i == j, across, 0), axis=1, keepdims=True)
     mine, other = (across, down) if axis == 0 else (down, across)
     before = (other < mine) | ((other == mine) & (j < i))
     return jnp.sum(before.astype(jnp.int32), axis=axis, keepdims=True)
@@ -75,10 +76,10 @@
     return inner, pair, stays, here
 
 
-def picking_kernel(owner_count, across, down, expert_owner, picks):
+def picking_kernel(owner_count, across, expert_owner, picks):
     per_owner = TILE // owner_count
     block_count = picks.shape[0] // TILE
-    rank = ranks(across[...], down[...], 0)
+    rank = ranks(across[...], 0)
     place = lax.broadcasted_iota(jnp.int32, (HALF, TILE), 0)
     for block in range(block_count):
         inner, pair, stays, _ = owners_of(rank, block, expert_owner, owner_count, block_count)
@@ -91,7 +92,6 @@
 def placing_kernel(
     owner_count,
     across,
-    down,
     expert_owner,
     core,
     back_go,
@@ -106,8 +106,8 @@
     row_count = back_go.shape[0]
     block_count = row_count // TILE
     chunk_rows = row_count // 2
-    along = ranks(across[...], down[...], 0)
-    upright = ranks(across[...], down[...], 1)
+    along = ranks(across[...], 0)
+    upright = ranks(across[...], 1)
     lanes = lax.broadcasted_iota(jnp.int32, (TILE, chunk_rows), 1)
     sublanes = lax.broadcasted_iota(jnp.int32, (row_count, TILE), 0)
     for block in range(block_count):
@@ -185,8 +185,8 @@
     return total
 
 
-def sending_kernel(bit, chunk, kept, *rest):
-    later, out = rest[:-1], rest[-1]
+def sending_kernel(bit, chunk, count, kept, *rest):
+    later, out = rest[:count], rest[-1]
     place = lax.axis_index("dp")
     low = place & ((1 << bit) - 1)
     other = (1 - ((place >> bit) & 1)) << bit
@@ -201,31 +201,45 @@
     parts[:, TILE:] = (total - high.astype(F32)).astype(BF16)
 
 
+def preparing_kernel(master, one, two, synced, pick, received, based, ones, twos, parts):
+    del received
+    based_all = master[...] * (1.0 - step_size * weight_decay) - synced[...].astype(F32)
+    for value, out in (
+        (based_all, based),
+        (beta_one * one[...], ones),
+        (beta_two * two[...], twos),
+    ):
+        in_two(value, parts)
+        pieces = jnp.dot(pick[...], parts[...], preferred_element_type=F32)
+        out[...] = pieces[:, :TILE] + pieces[:, TILE:]
+
+
 def going_kernel(steps, replica_count, kept, *rest):
     later = rest[:steps]
-    master, one, two, synced, record, back, pick, summed, outgoing, parts, clipped = rest[steps:]
-    in_two(sum_so_far(lax.axis_index("dp"), 0, kept, later), parts)
+    based, ones, twos, record, outgoing = rest[steps:]
+    gradient = sum_so_far(lax.axis_index("dp"), 0, kept, later) / replica_count
+    new_one = ones[...] + (1.0 - beta_one) * gradient
+    new_two = twos[...] + (1.0 - beta_two) * gradient * gradient
+    update = new_one / bias_one / (jnp.sqrt(new_two / bias_two) + adam_floor)
+    delta = based[...] - step_size * update
+    for tile in range(delta.shape[0] // HALF):
+        limit = record[0, tile]
+        rows = delta[tile * HALF : (tile + 1) * HALF]
+        outgoing[pl.ds(tile * HALF, HALF)] = jnp.clip(rows, -limit, limit).astype(BF16)
+
+
+def staying_kernel(steps, replica_count, kept, *rest):
+    go, stay, rest = rest[:steps], rest[steps : 2 * steps], rest[2 * steps :]
+    master, one, two, synced, record, back_go, back_stay, pack = rest[:8]
+    new_master, new_one, new_two, column_max, packed, parts_go, parts_stay, clipped = rest[8:]
+    place = lax.axis_index("dp")
+    in_two(sum_so_far(place, 0, kept, go), parts_go)
+    in_two(sum_so_far(place, 1, kept, stay), parts_stay)
     for tile in range(master.shape[0] // TILE):
         at = pl.ds(tile * TILE, TILE)
-        pieces = jnp.dot(back[at], parts[...], preferred_element_type=F32)
+        pieces = jnp.dot(back_go[at], parts_go[...], preferred_element_type=F32)
+        pieces = pieces + jnp.dot(back_stay[at], parts_stay[...], preferred_element_type=F32)
         total = pieces[:, :TILE] + pieces[:, TILE:]
-        summed[at] = total
-        updated, _, _ = adam_step(master[at], one[at], two[at], total / replica_count)
-        delta = updated - synced[at].astype(F32)
-        limit = record[0, tile]
-        clipped[at] = jnp.clip(delta, -limit, limit).astype(BF16)
-    outgoing[...] = jnp.dot(pick[...], clipped[...], preferred_element_type=F32).astype(BF16)
-
-
-def staying_kernel(steps, replica_count, kept, *rest):
-    later = rest[:steps]
-    master, one, two, synced, record, back, pack, summed = rest[steps : steps + 8]
-    new_master, new_one, new_two, column_max, packed, parts, clipped = rest[steps + 8 :]
-    in_two(sum_so_far(lax.axis_index("dp"), 1, kept, later), parts)
-    for tile in range(master.shape[0] // TILE):
-        at = pl.ds(tile * TILE, TILE)
-        pieces = jnp.dot(back[at], parts[...], preferred_element_type=F32)
-        total = summed[at] + (pieces[:, :TILE] + pieces[:, TILE:])
         a, b, c = adam_step(master[at], one[at], two[at], total / replica_count)
         new_master[at] = a
         new_one[at] = b
@@ -268,8 +282,8 @@
         [gradients],
         [pltpu.SemaphoreType.DMA((replica_count // 2,))],
     )
-    table = [row_table.reshape(1, TILE), row_table.reshape(TILE, 1), expert_owner]
-    table_specs = [VMEM, VMEM, SMEM]
+    table = [row_table.reshape(1, TILE), expert_owner]
+    table_specs = [VMEM, SMEM]
     picks = call(
         functools.partial(picking_kernel, owner_count), shape(row_count, TILE), table_specs, table
     )
@@ -306,34 +320,48 @@
         [*summands, kept, pick_go],
     )
     later[1].append(exchange(second, "dp", 2, replica_count))
+    state = [master, moment_one, moment_two, synced]
+    record = amax_record.reshape(1, block_count)
+    going = shape(rows, TILE, dtype=F32)
     for bit in range(2, steps + 1):
         for chunk in range(2):
+            ahead = []
+            if bit == 2 and chunk == 1:
+                prepared = call(
+                    preparing_kernel,
+                    (going, going, going),
+                    [VMEM] * 5 + [ANY],
+                    [*state, pick_go, later[0][0]],
+                    [pltpu.VMEM((row_count, 2 * TILE), BF16)],
+                )
+                ahead = [prepared[0]]
+            count = len(later[chunk])
             out = call(
-                functools.partial(sending_kernel, bit, chunk),
+                functools.partial(sending_kernel, bit, chunk, count),
                 shape(replica_count >> (bit + 1), rows, TILE),
-                [VMEM] * (1 + len(later[chunk])),
-                [kept, *later[chunk]],
+                [VMEM] * (1 + count) + [ANY] * len(ahead),
+                [kept, *later[chunk], *ahead],
             )
             later[chunk].append(exchange(out, "dp", 1 << bit, replica_count))
 
-    state = [master, moment_one, moment_two, synced, amax_record.reshape(1, block_count)]
-    state_specs = [VMEM] * 4 + [SMEM]
-    scratch = [pltpu.VMEM((rows, 2 * TILE), BF16), pltpu.VMEM((row_count, TILE), BF16)]
-    summed, outgoing = call(
+    outgoing = call(
         functools.partial(going_kernel, steps, replica_count),
-        (shape(row_count, TILE, dtype=F32), shape(rows, TILE)),
-        [VMEM] * (1 + steps) + state_specs + [VMEM] * 2,
-        [kept, *later[0], *state, back_go, pick_go],
-        scratch,
+        shape(rows, TILE),
+        [VMEM] * (1 + steps + 3) + [SMEM],
+        [kept, *later[0], *prepared, record],
     )
     arrived = exchange(outgoing, "fsdp", half, owner_count)
     full = shape(row_count, TILE, dtype=F32)
     new_master, new_one, new_two, column_max, packed = call(
         functools.partial(staying_kernel, steps, replica_count),
         (full, full, full, shape(block_count, TILE, dtype=F32), shape(row_count, TILE)),
-        [VMEM] * (1 + steps) + state_specs + [VMEM] * 3,
-        [kept, *later[1], *state, back_stay, pack_stay, summed],
-        scratch,
+        [VMEM] * (1 + 2 * steps + 4) + [SMEM] + [VMEM] * 3,
+        [kept, *later[0], *later[1], *state, record, back_go, back_stay, pack_stay],
+        [
+            pltpu.VMEM((rows, 2 * TILE), BF16),
+            pltpu.VMEM((rows, 2 * TILE), BF16),
+            pltpu.VMEM((row_count, TILE), BF16),
+        ],
     )
     new_amax = jnp.max(column_max, axis=1).reshape(block_count, 1)
     packed = call(

time: 82.4 us -> 80.7 us (0.979)
  starting transfers between devices: 59.5 us -> 57.8 us
    all_to_all x1, starting transfers between devices: 11.5 us -> 10.5 us  [body(): lax.all_to_all(packed.reshape(row_count // 2, 2, TILE), 'fsdp', split_axi...]
    pallas_call x14 -> x15, Pallas kernels: 7.84 us -> 8.01 us  [call(): pl.pallas_call(kernel, out_shape=outs, in_specs=ins, out_specs=VMEM if si...]
  transfers between devices with their start and end apart: 9 -> 9, of which waited for: 5 -> 4; matrix products, arithmetic and copies ran while one was open for 2% -> 1% of each run, Pallas kernels for 7% -> 7%
where the time goes in v5:
time: 80.7 us; the launch traced here: 80.2 us
  starting transfers between devices  57.8 us (72%)
  waiting for transfers between devices  11.1 us (14%)
  Pallas kernels  8.01 us (10%)
  local copies, waits for them, and re-layouts  1.8 us (2%)
  between operations  0.93 us (1%)
    ppermute x8, starting transfers between devices, exchange(): return lax.ppermute(x, axis, [(i, i ^ distance) for i in range(count)])  47.3 us
    all_to_all x1, starting transfers between devices, body(): lax.all_to_all(packed.reshape(row_count // 2, 2, TILE), 'fsdp', split_axi...  10.5 us
    all_to_all x1, waiting for transfers between devices, body(): lax.all_to_all(packed.reshape(row_count // 2, 2, TILE), 'fsdp', split_axi...  8.77 us
    pallas_call x15, Pallas kernels, call(): pl.pallas_call(kernel, out_shape=outs, in_specs=ins, out_specs=VMEM if si...  8.01 us
    ppermute x8, waiting for transfers between devices, exchange(): return lax.ppermute(x, axis, [(i, i ^ distance) for i in range(count)])  2.32 us
    unnamed x18, local copies, waits for them, and re-layouts  1.8 us
  transfers between devices with their start and end apart: 9, of which 4 were waited for; matrix products, arithmetic and copies ran while one was open for 1% of the time, Pallas kernels for 7%

profile of v5, /device:TPU:8, one launch (start us, length us, event | category | flops | bytes accessed | tf_op | source)
XLA Modules:
  0.0 80.2 jit_solution(16790446508346137327)
XLA Ops:
  0.6 1.9 %collective-permute-start = (bf16[1,384,2048]{2,1,0:T(8,128)(2,1)}, bf16[1,384,2048]{2,1,0:T(8,128)(2,1)S(1)}, u32[]{:S(2)}, u32[]{:S(2)}) collective-permute-start(bf16[1,384,2048]{2,1,0:T(8,128)(2,1)} %gradients.1), channel_id=1, source_target_pairs={{0,64},{64,0},{128,192},{192,128},{256,320},{320,256},{384,448},{4... | collective-permute-start | bytes 4718600 | tf_op jit(solution)/shard_map/ppermute | solution.py:53
  2.6 1.4 %copy-done = bf16[1,384,2048]{2,1,0:T(8,128)(2,1)S(1)} copy-done((bf16[1,384,2048]{2,1,0:T(8,128)(2,1)S(1)}, bf16[1,384,2048]{2,1,0:T(8,128)(2,1)}, u32[]{:S(2)}) %copy-start) | copy-done | bytes 1572888
  4.0 0.3 shard_map.128.own
  4.3 0.3 copy-done.6
  4.6 0.7 shard_map.129.picks
  5.3 0.8 %collective-permute-done.core = bf16[1,384,2048]{2,1,0:T(8,128)(2,1)S(1)} collective-permute-done((bf16[1,384,2048]{2,1,0:T(8,128)(2,1)}, bf16[1,384,2048]{2,1,0:T(8,128)(2,1)S(1)}, u32[]{:S(2)}, u32[]{:S(2)}) %collective-permute-start) | collective-permute-done | bytes 1572896 | tf_op jit(solution)/shard_map/ppermute | solution.py:53
  6.4 4.3 %collective-permute-start.1 = (bf16[4,192,128]{2,1,0:T(8,128)(2,1)S(1)}, bf16[4,192,128]{2,1,0:T(8,128)(2,1)S(1)}, u32[]{:S(2)}, u32[]{:S(2)}) collective-permute-start(bf16[4,192,128]{2,1,0:T(8,128)(2,1)S(1)} %shard_map.131), channel_id=1, source_target_pairs={{0,128},{64,192},{128,0},{192,64},{256,384},{320,448},{384,256},{4... | collective-permute-start | bytes 589832 | tf_op jit(solution)/shard_map/ppermute | solution.py:53
  10.7 0.3 shard_map.130.kept.rest_0_
  11.0 1.3 %shard_map.134 = (bf16[384,192]{1,0:T(8,128)(2,1)S(1)}, bf16[384,192]{1,0:T(8,128)(2,1)S(1)}, bf16[192,384]{1,0:T(8,128)(2,1)S(1)}, bf16[384,384]{1,0:T(8,128)(2...) custom-call(s32[1,128]{1,0:T(1,128)S(1)} %bitcast.7, s32[4]{0:T(128)S(1)} %copy-done.7, ...), custom_call_target="tpu_custom_call" | custom-call | flops 1048576 | bytes 1048576 | tf_op jit(solution)/shard_map/pallas_call | solution.py:39
  12.7 1.9 %collective-permute-start.4 = (bf16[4,192,128]{2,1,0:T(8,128)(2,1)S(1)}, bf16[4,192,128]{2,1,0:T(8,128)(2,1)S(1)}, u32[]{:S(2)}, u32[]{:S(2)}) collective-permute-start(bf16[4,192,128]{2,1,0:T(8,128)(2,1)S(1)} %shard_map.135), channel_id=1, source_target_pairs={{0,128},{64,192},{128,0},{192,64},{256,384},{320,448},{384,256},{4... | collective-permute-start | bytes 589832 | tf_op jit(solution)/shard_map/ppermute | solution.py:53
  14.6 1.3 %collective-permute-done.1.rest_0_.received = bf16[4,192,128]{2,1,0:T(8,128)(2,1)S(1)} collective-permute-done((bf16[4,192,128]{2,1,0:T(8,128)(2,1)S(1)}, bf16[4,192,128]{2,1,0:T(8,128)(2,1)S(1)}, u32[]{:S(2)}, u32[]{:S(2)}) %collective-permute-start.1) | collective-permute-done | bytes 196640 | tf_op jit(solution)/shard_map/ppermute | solution.py:53
  15.9 6.1 %collective-permute-start.2 = (bf16[2,192,128]{2,1,0:T(8,128)(2,1)S(1)}, bf16[2,192,128]{2,1,0:T(8,128)(2,1)S(1)}, u32[]{:S(2)}, u32[]{:S(2)}) collective-permute-start(bf16[2,192,128]{2,1,0:T(8,128)(2,1)S(1)} %shard_map.132), channel_id=1, source_target_pairs={{0,256},{64,320},{128,384},{192,448},{256,0},{320,64},{384,128},{4... | collective-permute-start | bytes 294920 | tf_op jit(solution)/shard_map/ppermute | solution.py:53
  22.1 0.4 shard_map.136
  22.6 5.8 %collective-permute-start.5 = (bf16[2,192,128]{2,1,0:T(8,128)(2,1)S(1)}, bf16[2,192,128]{2,1,0:T(8,128)(2,1)S(1)}, u32[]{:S(2)}, u32[]{:S(2)}) collective-permute-start(bf16[2,192,128]{2,1,0:T(8,128)(2,1)S(1)} %shard_map.137), channel_id=1, source_target_pairs={{0,256},{64,320},{128,384},{192,448},{256,0},{320,64},{384,128},{4... | collective-permute-start | bytes 294920 | tf_op jit(solution)/shard_map/ppermute | solution.py:53
  28.5 10.9 %collective-permute-start.3 = (bf16[1,192,128]{2,1,0:T(8,128)(2,1)S(1)}, bf16[1,192,128]{2,1,0:T(8,128)(2,1)S(1)}, u32[]{:S(2)}, u32[]{:S(2)}) collective-permute-start(bf16[1,192,128]{2,1,0:T(8,128)(2,1)S(1)} %shard_map.133), channel_id=1, source_target_pairs={{0,512},{64,576},{128,640},{192,704},{256,768},{320,832},{384,896}... | collective-permute-start | bytes 147464 | tf_op jit(solution)/shard_map/ppermute | solution.py:53
  39.4 3.7 %collective-permute-start.6 = (bf16[1,192,128]{2,1,0:T(8,128)(2,1)S(1)}, bf16[1,192,128]{2,1,0:T(8,128)(2,1)S(1)}, u32[]{:S(2)}, u32[]{:S(2)}) collective-permute-start(bf16[1,192,128]{2,1,0:T(8,128)(2,1)S(1)} %shard_map.138), channel_id=1, source_target_pairs={{0,512},{64,576},{128,640},{192,704},{256,768},{320,832},{384,896}... | collective-permute-start | bytes 147464 | tf_op jit(solution)/shard_map/ppermute | solution.py:53
  43.1 0.7 shard_map.140
  43.8 12.7 %collective-permute-start.7 = (bf16[192,128]{1,0:T(8,128)(2,1)S(1)}, bf16[192,128]{1,0:T(8,128)(2,1)S(1)}, u32[]{:S(2)}, u32[]{:S(2)}) collective-permute-start(bf16[192,128]{1,0:T(8,128)(2,1)S(1)} %shard_map.140), channel_id=1, source_target_pairs={{0,32},{1,33},{2,34},{3,35},{4,36},{5,37},{6,38},{7,39},{8,40},{9,... | collective-permute-start | bytes 147464 | tf_op jit(solution)/shard_map/ppermute | solution.py:53
  56.6 1.9 %shard_map.139 = (f32[384,128]{1,0:T(8,128)}, f32[384,128]{1,0:T(8,128)}, f32[384,128]{1,0:T(8,128)}, f32[3,128]{1,0:T(4,128)S(1)}, bf16[384,128]{1,0:T(8,128)(2,1)S(1)}) custom-call(bf16[4,384,128]{2,1,0:T(8,128)(2,1)S(1)} %shard_map.130.kept.rest_0_, bf16[4,192,128]{2,1,0:T(8,128)(2,1)S(1)} %collective-permute-done.1.rest_0_.received, ...), custom_call_target="tpu_custom_call" | custom-call | flops 1048576 | bytes 1048576 | tf_op jit(solution)/shard_map/pallas_call | solution.py:39
  58.6 0.8 %shard_map.141 = bf16[384,128]{1,0:T(8,128)(2,1)} custom-call(bf16[192,128]{1,0:T(8,128)(2,1)S(1)} %collective-permute-done.7.arrived, bf16[384,192]{1,0:T(8,128)(2,1)S(1)} %get-tuple-element.30.pack, bf16[384,128]{1,0:T(8,128)(2,1)S(1)} %get-tuple-element.31.staying), custom_call_target="tpu_custom_call" | custom-call | flops 1048576 | bytes 1048576 | tf_op jit(solution)/shard_map/pallas_call | solution.py:39
  59.5 10.5 %all-to-all-start = ((bf16[192,2,128]{2,1,0:T(2,128)(2,1)}), bf16[192,2,128]{2,1,0:T(2,128)(2,1)S(1)}, u32[]{:S(2)}, u32[]{:S(2)}) async-start(bf16[192,2,128]{2,1,0:T(2,128)(2,1)} %bitcast.3), calls=%async_computation | async-start | bytes 196608 | tf_op jit(solution)/shard_map/all_to_all | solution.py:373
  70.0 0.6 reduce_max.9
  70.6 8.8 %all-to-all-done = bf16[192,2,128]{2,1,0:T(2,128)(2,1)S(1)} async-done(((bf16[192,2,128]{2,1,0:T(2,128)(2,1)}), bf16[192,2,128]{2,1,0:T(2,128)(2,1)S(1)}, u32[]{:S(2)}, u32[]{:S(2)}) %all-to-all-start) | async-done | bytes 98336 | tf_op jit(solution)/shard_map/all_to_all | solution.py:373
  79.4 0.9 %shard_map.142 = bf16[384,128]{1,0:T(8,128)(2,1)} custom-call(bf16[384,128]{1,0:T(8,128)(2,1)S(1)} %bitcast.5, bf16[384,384]{1,0:T(8,128)(2,1)S(1)} %get-tuple-element.32.order, bf16[384,128]{1,0:T(8,128)(2,1)S(1)} %copy-done.5), custom_call_target="tpu_custom_call" | custom-call | flops 1048576 | bytes 1048576 | tf_op jit(solution)/shard_map/pallas_call | solution.py:39
  (28 shorter events, 1.0 us)
Async XLA Ops:
  0.6 5.5 %collective-permute-start = (bf16[1,384,2048]{2,1,0:T(8,128)(2,1)}, bf16[1,384,2048]{2,1,0:T(8,128)(2,1)S(1)}, u32[]{:S(2)}, u32[]{:S(2)}) collective-permute-start(bf16[1,384,2048]{2,1,0:T(8,128)(2,1)} %gradients.1), channel_id=1, source_target_pairs={{0,64},{64,0},{128,192},{192,128},{256,320},{320,256},{384,448},{4... | collective-permute-start | bytes 4718600 | tf_op jit(solution)/shard_map/ppermute | solution.py:53
  2.6 1.4 %copy-start = (bf16[1,384,2048]{2,1,0:T(8,128)(2,1)S(1)}, bf16[1,384,2048]{2,1,0:T(8,128)(2,1)}, u32[]{:S(2)}) copy-start(bf16[1,384,2048]{2,1,0:T(8,128)(2,1)} %gradients.1) | copy-start | bytes 4718596
  4.0 0.7 copy-start.6
  4.0 0.7 copy-start.7
  6.4 9.5 %collective-permute-start.1 = (bf16[4,192,128]{2,1,0:T(8,128)(2,1)S(1)}, bf16[4,192,128]{2,1,0:T(8,128)(2,1)S(1)}, u32[]{:S(2)}, u32[]{:S(2)}) collective-permute-start(bf16[4,192,128]{2,1,0:T(8,128)(2,1)S(1)} %shard_map.131), channel_id=1, source_target_pairs={{0,128},{64,192},{128,0},{192,64},{256,384},{320,448},{384,256},{4... | collective-permute-start | bytes 589832 | tf_op jit(solution)/shard_map/ppermute | solution.py:53
  12.3 9.7 %copy-start.1 = (f32[384,128]{1,0:T(8,128)S(1)}, f32[384,128]{1,0:T(8,128)}, u32[]{:S(2)}) copy-start(f32[384,128]{1,0:T(8,128)} %rest_6_.1) | copy-start | bytes 589828
  12.3 9.7 %copy-start.2 = (f32[384,128]{1,0:T(8,128)S(1)}, f32[384,128]{1,0:T(8,128)}, u32[]{:S(2)}) copy-start(f32[384,128]{1,0:T(8,128)} %rest_7_.1) | copy-start | bytes 589828
  12.3 9.7 %copy-start.3 = (f32[384,128]{1,0:T(8,128)S(1)}, f32[384,128]{1,0:T(8,128)}, u32[]{:S(2)}) copy-start(f32[384,128]{1,0:T(8,128)} %rest_8_.1) | copy-start | bytes 589828
  12.4 9.7 %copy-start.4 = (bf16[384,128]{1,0:T(8,128)(2,1)S(1)}, bf16[384,128]{1,0:T(8,128)(2,1)}, u32[]{:S(2)}) copy-start(bf16[384,128]{1,0:T(8,128)(2,1)} %rest_9_.1) | copy-start | bytes 294916
  12.7 9.9 %collective-permute-start.4 = (bf16[4,192,128]{2,1,0:T(8,128)(2,1)S(1)}, bf16[4,192,128]{2,1,0:T(8,128)(2,1)S(1)}, u32[]{:S(2)}, u32[]{:S(2)}) collective-permute-start(bf16[4,192,128]{2,1,0:T(8,128)(2,1)S(1)} %shard_map.135), channel_id=1, source_target_pairs={{0,128},{64,192},{128,0},{192,64},{256,384},{320,448},{384,256},{4... | collective-permute-start | bytes 589832 | tf_op jit(solution)/shard_map/ppermute | solution.py:53
  15.9 27.2 %copy-start.8 = (f32[3,1]{0,1:T(1,128)S(1)}, f32[3,1]{0,1:T(1,128)}, u32[]{:S(2)}) copy-start(f32[3,1]{0,1:T(1,128)} %param.15) | copy-start | bytes 40
  15.9 12.5 %collective-permute-start.2 = (bf16[2,192,128]{2,1,0:T(8,128)(2,1)S(1)}, bf16[2,192,128]{2,1,0:T(8,128)(2,1)S(1)}, u32[]{:S(2)}, u32[]{:S(2)}) collective-permute-start(bf16[2,192,128]{2,1,0:T(8,128)(2,1)S(1)} %shard_map.132), channel_id=1, source_target_pairs={{0,256},{64,320},{128,384},{192,448},{256,0},{320,64},{384,128},{4... | collective-permute-start | bytes 294920 | tf_op jit(solution)/shard_map/ppermute | solution.py:53
  22.6 16.8 %collective-permute-start.5 = (bf16[2,192,128]{2,1,0:T(8,128)(2,1)S(1)}, bf16[2,192,128]{2,1,0:T(8,128)(2,1)S(1)}, u32[]{:S(2)}, u32[]{:S(2)}) collective-permute-start(bf16[2,192,128]{2,1,0:T(8,128)(2,1)S(1)} %shard_map.137), channel_id=1, source_target_pairs={{0,256},{64,320},{128,384},{192,448},{256,0},{320,64},{384,128},{4... | collective-permute-start | bytes 294920 | tf_op jit(solution)/shard_map/ppermute | solution.py:53
  28.5 14.7 %collective-permute-start.3 = (bf16[1,192,128]{2,1,0:T(8,128)(2,1)S(1)}, bf16[1,192,128]{2,1,0:T(8,128)(2,1)S(1)}, u32[]{:S(2)}, u32[]{:S(2)}) collective-permute-start(bf16[1,192,128]{2,1,0:T(8,128)(2,1)S(1)} %shard_map.133), channel_id=1, source_target_pairs={{0,512},{64,576},{128,640},{192,704},{256,768},{320,832},{384,896}... | collective-permute-start | bytes 147464 | tf_op jit(solution)/shard_map/ppermute | solution.py:53
  39.4 17.1 %collective-permute-start.6 = (bf16[1,192,128]{2,1,0:T(8,128)(2,1)S(1)}, bf16[1,192,128]{2,1,0:T(8,128)(2,1)S(1)}, u32[]{:S(2)}, u32[]{:S(2)}) collective-permute-start(bf16[1,192,128]{2,1,0:T(8,128)(2,1)S(1)} %shard_map.138), channel_id=1, source_target_pairs={{0,512},{64,576},{128,640},{192,704},{256,768},{320,832},{384,896}... | collective-permute-start | bytes 147464 | tf_op jit(solution)/shard_map/ppermute | solution.py:53
  43.8 35.5 %copy-start.5 = (bf16[384,128]{1,0:T(8,128)(2,1)S(1)}, bf16[384,128]{1,0:T(8,128)(2,1)}, u32[]{:S(2)}) copy-start(bf16[384,128]{1,0:T(8,128)(2,1)} %rollout.1) | copy-start | bytes 294916
  43.8 14.8 %collective-permute-start.7 = (bf16[192,128]{1,0:T(8,128)(2,1)S(1)}, bf16[192,128]{1,0:T(8,128)(2,1)S(1)}, u32[]{:S(2)}, u32[]{:S(2)}) collective-permute-start(bf16[192,128]{1,0:T(8,128)(2,1)S(1)} %shard_map.140), channel_id=1, source_target_pairs={{0,32},{1,33},{2,34},{3,35},{4,36},{5,37},{6,38},{7,39},{8,40},{9,... | collective-permute-start | bytes 147464 | tf_op jit(solution)/shard_map/ppermute | solution.py:53
  59.5 19.9 %all-to-all-start = ((bf16[192,2,128]{2,1,0:T(2,128)(2,1)}), bf16[192,2,128]{2,1,0:T(2,128)(2,1)S(1)}, u32[]{:S(2)}, u32[]{:S(2)}) async-start(bf16[192,2,128]{2,1,0:T(2,128)(2,1)} %bitcast.3), calls=%async_computation | async-start | bytes 196608 | tf_op jit(solution)/shard_map/all_to_all | solution.py:373

commit v6 on v5

--- a/solution.py
+++ b/solution.py
@@ -313,19 +313,14 @@
         [*table_specs, ANY],
         [*table, core],
     )
-    second = call(
-        functools.partial(first_kernel, True, (1,)),
-        sent,
-        [VMEM] * 3 + [ANY] * 2,
-        [*summands, kept, pick_go],
-    )
+    second = call(functools.partial(first_kernel, True, (1,)), sent, [VMEM] * 3, summands)
     later[1].append(exchange(second, "dp", 2, replica_count))
     state = [master, moment_one, moment_two, synced]
     record = amax_record.reshape(1, block_count)
     going = shape(rows, TILE, dtype=F32)
     for bit in range(2, steps + 1):
         for chunk in range(2):
-            ahead = []
+            ahead = [pick_go] if bit == 2 else []
             if bit == 2 and chunk == 1:
                 prepared = call(
                     preparing_kernel,

time: 80.7 us -> 82.2 us (1.019)
    all_to_all x1, starting transfers between devices: 10.5 us -> 12 us  [body(): lax.all_to_all(packed.reshape(row_count // 2, 2, TILE), 'fsdp', split_axi...]
  transfers between devices with their start and end apart: 9 -> 9, of which waited for: 4 -> 5; matrix products, arithmetic and copies ran while one was open for 1% -> 1% of each run, Pallas kernels for 7% -> 7%
where the time goes in v6:
time: 82.2 us; the launch traced here: 81.8 us
  starting transfers between devices  58.6 us (71%)
  waiting for transfers between devices  11.9 us (14%)
  Pallas kernels  7.97 us (10%)
  local copies, waits for them, and re-layouts  1.8 us (2%)
  between operations  0.91 us (1%)
    ppermute x8, starting transfers between devices, exchange(): return lax.ppermute(x, axis, [(i, i ^ distance) for i in range(count)])  46.5 us
    all_to_all x1, starting transfers between devices, body(): lax.all_to_all(packed.reshape(row_count // 2, 2, TILE), 'fsdp', split_axi...  12 us
    all_to_all x1, waiting for transfers between devices, body(): lax.all_to_all(packed.reshape(row_count // 2, 2, TILE), 'fsdp', split_axi...  8.77 us
    pallas_call x15, Pallas kernels, call(): pl.pallas_call(kernel, out_shape=outs, in_specs=ins, out_specs=VMEM if si...  7.97 us
    ppermute x8, waiting for transfers between devices, exchange(): return lax.ppermute(x, axis, [(i, i ^ distance) for i in range(count)])  3.13 us
    unnamed x18, local copies, waits for them, and re-layouts  1.8 us
  transfers between devices with their start and end apart: 9, of which 5 were waited for; matrix products, arithmetic and copies ran while one was open for 1% of the time, Pallas kernels for 7%

profile of v6, /device:TPU:8, one launch (start us, length us, event | category | flops | bytes accessed | tf_op | source)
XLA Modules:
  0.0 81.8 jit_solution(14242742135248666358)
XLA Ops:
  0.6 1.9 %collective-permute-start = (bf16[1,384,2048]{2,1,0:T(8,128)(2,1)}, bf16[1,384,2048]{2,1,0:T(8,128)(2,1)S(1)}, u32[]{:S(2)}, u32[]{:S(2)}) collective-permute-start(bf16[1,384,2048]{2,1,0:T(8,128)(2,1)} %gradients.1), channel_id=1, source_target_pairs={{0,64},{64,0},{128,192},{192,128},{256,320},{320,256},{384,448},{4... | collective-permute-start | bytes 4718600 | tf_op jit(solution)/shard_map/ppermute | solution.py:53
  2.6 1.4 %copy-done = bf16[1,384,2048]{2,1,0:T(8,128)(2,1)S(1)} copy-done((bf16[1,384,2048]{2,1,0:T(8,128)(2,1)S(1)}, bf16[1,384,2048]{2,1,0:T(8,128)(2,1)}, u32[]{:S(2)}) %copy-start) | copy-done | bytes 1572888
  4.3 0.3 copy-done.6
  4.6 0.7 shard_map.129.picks
  5.3 0.8 collective-permute-done.core
  6.4 4.3 %collective-permute-start.1 = (bf16[4,192,128]{2,1,0:T(8,128)(2,1)S(1)}, bf16[4,192,128]{2,1,0:T(8,128)(2,1)S(1)}, u32[]{:S(2)}, u32[]{:S(2)}) collective-permute-start(bf16[4,192,128]{2,1,0:T(8,128)(2,1)S(1)} %shard_map.131), channel_id=1, source_target_pairs={{0,128},{64,192},{128,0},{192,64},{256,384},{320,448},{384,256},{4... | collective-permute-start | bytes 589832 | tf_op jit(solution)/shard_map/ppermute | solution.py:53
  11.0 1.9 %collective-permute-start.4 = (bf16[4,192,128]{2,1,0:T(8,128)(2,1)S(1)}, bf16[4,192,128]{2,1,0:T(8,128)(2,1)S(1)}, u32[]{:S(2)}, u32[]{:S(2)}) collective-permute-start(bf16[4,192,128]{2,1,0:T(8,128)(2,1)S(1)} %shard_map.135), channel_id=1, source_target_pairs={{0,128},{64,192},{128,0},{192,64},{256,384},{320,448},{384,256},{4... | collective-permute-start | bytes 589832 | tf_op jit(solution)/shard_map/ppermute | solution.py:53
  12.9 0.3 shard_map.130.kept
  13.3 1.3 %shard_map.132 = (bf16[384,192]{1,0:T(8,128)(2,1)S(1)}, bf16[384,192]{1,0:T(8,128)(2,1)S(1)}, bf16[192,384]{1,0:T(8,128)(2,1)S(1)}, bf16[384,384]{1,0:T(8,128)(2...) custom-call(s32[1,128]{1,0:T(1,128)S(1)} %bitcast.7, s32[4]{0:T(128)S(1)} %copy-done.7, ...), custom_call_target="tpu_custom_call" | custom-call | flops 1048576 | bytes 1048576 | tf_op jit(solution)/shard_map/pallas_call | solution.py:39
  14.6 1.8 %collective-permute-done.1.rest_0_.received = bf16[4,192,128]{2,1,0:T(8,128)(2,1)S(1)} collective-permute-done((bf16[4,192,128]{2,1,0:T(8,128)(2,1)S(1)}, bf16[4,192,128]{2,1,0:T(8,128)(2,1)S(1)}, u32[]{:S(2)}, u32[]{:S(2)}) %collective-permute-start.1) | collective-permute-done | bytes 196640 | tf_op jit(solution)/shard_map/ppermute | solution.py:53
  16.4 6.1 %collective-permute-start.2 = (bf16[2,192,128]{2,1,0:T(8,128)(2,1)S(1)}, bf16[2,192,128]{2,1,0:T(8,128)(2,1)S(1)}, u32[]{:S(2)}, u32[]{:S(2)}) collective-permute-start(bf16[2,192,128]{2,1,0:T(8,128)(2,1)S(1)} %shard_map.133), channel_id=1, source_target_pairs={{0,256},{64,320},{128,384},{192,448},{256,0},{320,64},{384,128},{4... | collective-permute-start | bytes 294920 | tf_op jit(solution)/shard_map/ppermute | solution.py:53
  22.6 0.4 shard_map.136
  23.1 3.5 %collective-permute-start.5 = (bf16[2,192,128]{2,1,0:T(8,128)(2,1)S(1)}, bf16[2,192,128]{2,1,0:T(8,128)(2,1)S(1)}, u32[]{:S(2)}, u32[]{:S(2)}) collective-permute-start(bf16[2,192,128]{2,1,0:T(8,128)(2,1)S(1)} %shard_map.137), channel_id=1, source_target_pairs={{0,256},{64,320},{128,384},{192,448},{256,0},{320,64},{384,128},{4... | collective-permute-start | bytes 294920 | tf_op jit(solution)/shard_map/ppermute | solution.py:53
  26.5 0.3 collective-permute-done.2.rest_1_
  26.9 10.9 %collective-permute-start.3 = (bf16[1,192,128]{2,1,0:T(8,128)(2,1)S(1)}, bf16[1,192,128]{2,1,0:T(8,128)(2,1)S(1)}, u32[]{:S(2)}, u32[]{:S(2)}) collective-permute-start(bf16[1,192,128]{2,1,0:T(8,128)(2,1)S(1)} %shard_map.134), channel_id=1, source_target_pairs={{0,512},{64,576},{128,640},{192,704},{256,768},{320,832},{384,896}... | collective-permute-start | bytes 147464 | tf_op jit(solution)/shard_map/ppermute | solution.py:53
  37.9 4.1 %collective-permute-start.6 = (bf16[1,192,128]{2,1,0:T(8,128)(2,1)S(1)}, bf16[1,192,128]{2,1,0:T(8,128)(2,1)S(1)}, u32[]{:S(2)}, u32[]{:S(2)}) collective-permute-start(bf16[1,192,128]{2,1,0:T(8,128)(2,1)S(1)} %shard_map.138), channel_id=1, source_target_pairs={{0,512},{64,576},{128,640},{192,704},{256,768},{320,832},{384,896}... | collective-permute-start | bytes 147464 | tf_op jit(solution)/shard_map/ppermute | solution.py:53
  42.1 0.7 shard_map.140
  42.8 13.8 %collective-permute-start.7 = (bf16[192,128]{1,0:T(8,128)(2,1)S(1)}, bf16[192,128]{1,0:T(8,128)(2,1)S(1)}, u32[]{:S(2)}, u32[]{:S(2)}) collective-permute-start(bf16[192,128]{1,0:T(8,128)(2,1)S(1)} %shard_map.140), channel_id=1, source_target_pairs={{0,32},{1,33},{2,34},{3,35},{4,36},{5,37},{6,38},{7,39},{8,40},{9,... | collective-permute-start | bytes 147464 | tf_op jit(solution)/shard_map/ppermute | solution.py:53
  56.6 1.9 %shard_map.139 = (f32[384,128]{1,0:T(8,128)}, f32[384,128]{1,0:T(8,128)}, f32[384,128]{1,0:T(8,128)}, f32[3,128]{1,0:T(4,128)S(1)}, bf16[384,128]{1,0:T(8,128)(2,1)S(1)}) custom-call(bf16[4,384,128]{2,1,0:T(8,128)(2,1)S(1)} %shard_map.130.kept, bf16[4,192,128]{2,1,0:T(8,128)(2,1)S(1)} %collective-permute-done.1.rest_0_.received, ...), custom_call_target="tpu_custom_call" | custom-call | flops 1048576 | bytes 1048576 | tf_op jit(solution)/shard_map/pallas_call | solution.py:39
  58.6 0.8 %shard_map.141 = bf16[384,128]{1,0:T(8,128)(2,1)} custom-call(bf16[192,128]{1,0:T(8,128)(2,1)S(1)} %collective-permute-done.7.arrived, bf16[384,192]{1,0:T(8,128)(2,1)S(1)} %get-tuple-element.30.pack, bf16[384,128]{1,0:T(8,128)(2,1)S(1)} %get-tuple-element.31.staying), custom_call_target="tpu_custom_call" | custom-call | flops 1048576 | bytes 1048576 | tf_op jit(solution)/shard_map/pallas_call | solution.py:39
  59.5 12.0 %all-to-all-start = ((bf16[192,2,128]{2,1,0:T(2,128)(2,1)}), bf16[192,2,128]{2,1,0:T(2,128)(2,1)S(1)}, u32[]{:S(2)}, u32[]{:S(2)}) async-start(bf16[192,2,128]{2,1,0:T(2,128)(2,1)} %bitcast.3), calls=%async_computation | async-start | bytes 196608 | tf_op jit(solution)/shard_map/all_to_all | solution.py:368
  71.5 0.6 reduce_max.9
  72.1 8.8 %all-to-all-done = bf16[192,2,128]{2,1,0:T(2,128)(2,1)S(1)} async-done(((bf16[192,2,128]{2,1,0:T(2,128)(2,1)}), bf16[192,2,128]{2,1,0:T(2,128)(2,1)S(1)}, u32[]{:S(2)}, u32[]{:S(2)}) %all-to-all-start) | async-done | bytes 98336 | tf_op jit(solution)/shard_map/all_to_all | solution.py:368
  80.9 0.9 %shard_map.142 = bf16[384,128]{1,0:T(8,128)(2,1)} custom-call(bf16[384,128]{1,0:T(8,128)(2,1)S(1)} %bitcast.5, bf16[384,384]{1,0:T(8,128)(2,1)S(1)} %get-tuple-element.32.order, bf16[384,128]{1,0:T(8,128)(2,1)S(1)} %copy-done.5), custom_call_target="tpu_custom_call" | custom-call | flops 1048576 | bytes 1048576 | tf_op jit(solution)/shard_map/pallas_call | solution.py:39
  (28 shorter events, 1.2 us)
Async XLA Ops:
  0.6 5.5 %collective-permute-start = (bf16[1,384,2048]{2,1,0:T(8,128)(2,1)}, bf16[1,384,2048]{2,1,0:T(8,128)(2,1)S(1)}, u32[]{:S(2)}, u32[]{:S(2)}) collective-permute-start(bf16[1,384,2048]{2,1,0:T(8,128)(2,1)} %gradients.1), channel_id=1, source_target_pairs={{0,64},{64,0},{128,192},{192,128},{256,320},{320,256},{384,448},{4... | collective-permute-start | bytes 4718600 | tf_op jit(solution)/shard_map/ppermute | solution.py:53
  2.6 1.4 %copy-start = (bf16[1,384,2048]{2,1,0:T(8,128)(2,1)S(1)}, bf16[1,384,2048]{2,1,0:T(8,128)(2,1)}, u32[]{:S(2)}) copy-start(bf16[1,384,2048]{2,1,0:T(8,128)(2,1)} %gradients.1) | copy-start | bytes 4718596
  4.0 0.7 copy-start.6
  4.0 0.7 copy-start.7
  6.4 10.0 %collective-permute-start.1 = (bf16[4,192,128]{2,1,0:T(8,128)(2,1)S(1)}, bf16[4,192,128]{2,1,0:T(8,128)(2,1)S(1)}, u32[]{:S(2)}, u32[]{:S(2)}) collective-permute-start(bf16[4,192,128]{2,1,0:T(8,128)(2,1)S(1)} %shard_map.131), channel_id=1, source_target_pairs={{0,128},{64,192},{128,0},{192,64},{256,384},{320,448},{384,256},{4... | collective-permute-start | bytes 589832 | tf_op jit(solution)/shard_map/ppermute | solution.py:53
  11.0 12.0 %collective-permute-start.4 = (bf16[4,192,128]{2,1,0:T(8,128)(2,1)S(1)}, bf16[4,192,128]{2,1,0:T(8,128)(2,1)S(1)}, u32[]{:S(2)}, u32[]{:S(2)}) collective-permute-start(bf16[4,192,128]{2,1,0:T(8,128)(2,1)S(1)} %shard_map.135), channel_id=1, source_target_pairs={{0,128},{64,192},{128,0},{192,64},{256,384},{320,448},{384,256},{4... | collective-permute-start | bytes 589832 | tf_op jit(solution)/shard_map/ppermute | solution.py:53
  13.3 9.3 %copy-start.1 = (f32[384,128]{1,0:T(8,128)S(1)}, f32[384,128]{1,0:T(8,128)}, u32[]{:S(2)}) copy-start(f32[384,128]{1,0:T(8,128)} %rest_6_.1) | copy-start | bytes 589828
  13.3 9.3 %copy-start.2 = (f32[384,128]{1,0:T(8,128)S(1)}, f32[384,128]{1,0:T(8,128)}, u32[]{:S(2)}) copy-start(f32[384,128]{1,0:T(8,128)} %rest_7_.1) | copy-start | bytes 589828
  13.3 9.3 %copy-start.3 = (f32[384,128]{1,0:T(8,128)S(1)}, f32[384,128]{1,0:T(8,128)}, u32[]{:S(2)}) copy-start(f32[384,128]{1,0:T(8,128)} %rest_8_.1) | copy-start | bytes 589828
  13.3 9.2 %copy-start.4 = (bf16[384,128]{1,0:T(8,128)(2,1)S(1)}, bf16[384,128]{1,0:T(8,128)(2,1)}, u32[]{:S(2)}) copy-start(bf16[384,128]{1,0:T(8,128)(2,1)} %rest_9_.1) | copy-start | bytes 294916
  16.4 25.6 %copy-start.8 = (f32[3,1]{0,1:T(1,128)S(1)}, f32[3,1]{0,1:T(1,128)}, u32[]{:S(2)}) copy-start(f32[3,1]{0,1:T(1,128)} %param.15) | copy-start | bytes 40
  16.4 10.5 %collective-permute-start.2 = (bf16[2,192,128]{2,1,0:T(8,128)(2,1)S(1)}, bf16[2,192,128]{2,1,0:T(8,128)(2,1)S(1)}, u32[]{:S(2)}, u32[]{:S(2)}) collective-permute-start(bf16[2,192,128]{2,1,0:T(8,128)(2,1)S(1)} %shard_map.133), channel_id=1, source_target_pairs={{0,256},{64,320},{128,384},{192,448},{256,0},{320,64},{384,128},{4... | collective-permute-start | bytes 294920 | tf_op jit(solution)/shard_map/ppermute | solution.py:53
  23.1 14.8 %collective-permute-start.5 = (bf16[2,192,128]{2,1,0:T(8,128)(2,1)S(1)}, bf16[2,192,128]{2,1,0:T(8,128)(2,1)S(1)}, u32[]{:S(2)}, u32[]{:S(2)}) collective-permute-start(bf16[2,192,128]{2,1,0:T(8,128)(2,1)S(1)} %shard_map.137), channel_id=1, source_target_pairs={{0,256},{64,320},{128,384},{192,448},{256,0},{320,64},{384,128},{4... | collective-permute-start | bytes 294920 | tf_op jit(solution)/shard_map/ppermute | solution.py:53
  26.9 15.1 %collective-permute-start.3 = (bf16[1,192,128]{2,1,0:T(8,128)(2,1)S(1)}, bf16[1,192,128]{2,1,0:T(8,128)(2,1)S(1)}, u32[]{:S(2)}, u32[]{:S(2)}) collective-permute-start(bf16[1,192,128]{2,1,0:T(8,128)(2,1)S(1)} %shard_map.134), channel_id=1, source_target_pairs={{0,512},{64,576},{128,640},{192,704},{256,768},{320,832},{384,896}... | collective-permute-start | bytes 147464 | tf_op jit(solution)/shard_map/ppermute | solution.py:53
  37.9 18.7 %collective-permute-start.6 = (bf16[1,192,128]{2,1,0:T(8,128)(2,1)S(1)}, bf16[1,192,128]{2,1,0:T(8,128)(2,1)S(1)}, u32[]{:S(2)}, u32[]{:S(2)}) collective-permute-start(bf16[1,192,128]{2,1,0:T(8,128)(2,1)S(1)} %shard_map.138), channel_id=1, source_target_pairs={{0,512},{64,576},{128,640},{192,704},{256,768},{320,832},{384,896}... | collective-permute-start | bytes 147464 | tf_op jit(solution)/shard_map/ppermute | solution.py:53
  42.7 38.1 %copy-start.5 = (bf16[384,128]{1,0:T(8,128)(2,1)S(1)}, bf16[384,128]{1,0:T(8,128)(2,1)}, u32[]{:S(2)}) copy-start(bf16[384,128]{1,0:T(8,128)(2,1)} %rollout.1) | copy-start | bytes 294916
  42.8 15.9 %collective-permute-start.7 = (bf16[192,128]{1,0:T(8,128)(2,1)S(1)}, bf16[192,128]{1,0:T(8,128)(2,1)S(1)}, u32[]{:S(2)}, u32[]{:S(2)}) collective-permute-start(bf16[192,128]{1,0:T(8,128)(2,1)S(1)} %shard_map.140), channel_id=1, source_target_pairs={{0,32},{1,33},{2,34},{3,35},{4,36},{5,37},{6,38},{7,39},{8,40},{9,... | collective-permute-start | bytes 147464 | tf_op jit(solution)/shard_map/ppermute | solution.py:53
  59.5 21.4 %all-to-all-start = ((bf16[192,2,128]{2,1,0:T(2,128)(2,1)}), bf16[192,2,128]{2,1,0:T(2,128)(2,1)S(1)}, u32[]{:S(2)}, u32[]{:S(2)}) async-start(bf16[192,2,128]{2,1,0:T(2,128)(2,1)} %bitcast.3), calls=%async_computation | async-start | bytes 196608 | tf_op jit(solution)/shard_map/all_to_all | solution.py:368
